TPU v7x, 128 devices: a whole 4x4x4 slice. The times are simulated.
128 devices in a mesh: section: 4 (over x), dp: 4 (over y), mp: 8 (over z, core).
Axes of the slice: x: 4, y: 4, z: 4, core: 2. Of those that a mesh axis runs over, the one named last changes fastest.
Arguments:
- patches: bfloat16 [1024, 5120], P('dp'), may hold values from -6 to 6
- ln_gain: float32 [1280], replicated, may hold values from 0.25 to 1.75
- ln_bias: float32 [1280], replicated, may hold values from -3 to 3
- w_merge_in: bfloat16 [5120, 5120], P(None, ('section', 'mp')), may hold values from -0.078125 to 0.078125
- b_merge_in: float32 [5120], P(('section', 'mp')), may hold values from -3 to 3
- w_merge_out: bfloat16 [5120, 8192], P(('section', 'mp')), may hold values from -0.15625 to 0.15625
- b_merge_out: float32 [8192], replicated, may hold values from -3 to 3
- text_rows: bfloat16 [4, 4, 128, 8192], P('section', 'dp', None, 'mp'), may hold values from -6 to 6
- section_gain: float32 [4, 8192], P('section'), may hold values from 0.1 to 1.9
- section_weight: bfloat16 [4, 8192, 8192], P('section', None, 'mp'), may hold values from -0.0625 to 0.0625
- image_sizes: int32 [4, 64], replicated, may hold values from 1 to 8, 256 in all within a row
- placement: int32 [4, 64], replicated, may hold values from 0 to 63, each once within a row
- offsets: int32 [4, 64], replicated, may hold values from 0 to 7
Outputs:
- final_stream: bfloat16 [4, 4, 128, 8192], P('section', 'dp', None, 'mp')
Inputs may be any that keep to these rules, and one draw needn't show every extreme that they name: `image_sizes`: each row sums to 256; the largest entry is exactly 8. `placement`: each row is a permutation, so each encoder group sends exactly 4 images to every owner.
All inputs are finite; a program needn't handle non-finite values.
Results may differ from a plain program's by a relative error of at most 0.02.
Values may be sent and summed in bfloat16 or wider, within the bound.
A program may use at most 128 MiB of HBM per device.

v0:
```python
import jax
import jax.numpy as jnp
from jax import lax
from jax.sharding import PartitionSpec as P

SLOT = 8
K_PAIR = 4


def passed_along(block, axis, distance):
    devices = range(lax.axis_size(axis))
    route = [(i - distance, i) for i in devices if i - distance in devices]
    return lax.ppermute(block, axis, route)


def slot_layout(image_sizes, placement, offsets, owners, k_pair, slot_len, rows_enc):
    targets = owners[:, None] * k_pair + jnp.arange(k_pair, dtype=jnp.int32)[None, :]
    matches = placement[:, None, None, :] == targets[None, :, :, None]
    starts = jnp.cumsum(image_sizes, axis=1) - image_sizes

    def picker(values):
        return jnp.sum(jnp.where(matches, values[:, None, None, :], 0), axis=-1)

    extent = picker(image_sizes)
    first_row = picker(starts)
    shift_in = jnp.minimum(picker(offsets), slot_len - extent)
    column = jnp.arange(slot_len, dtype=jnp.int32)
    inside = (column >= shift_in[..., None]) & (column < (shift_in + extent)[..., None])
    source = jnp.clip(first_row[..., None] + column - shift_in[..., None], 0, rows_enc - 1)
    return (source, inside)


def layer_norm(patches, ln_gain, ln_bias):
    values = patches.astype(jnp.float32).reshape(patches.shape[0], 4, -1)
    centre = values - jnp.mean(values, axis=-1, keepdims=True)
    spread = jnp.mean(centre * centre, axis=-1, keepdims=True)
    normed = centre * lax.rsqrt(spread + 1e-06) * ln_gain + ln_bias
    return normed.reshape(patches.shape[0], -1).astype(jnp.bfloat16)


def per_device(
    patches,
    ln_gain,
    ln_bias,
    w_merge_in,
    b_merge_in,
    w_merge_out,
    b_merge_out,
    text_rows,
    section_gain,
    section_weight,
    image_sizes,
    placement,
    offsets,
):
    n_section = lax.axis_size("section")
    n_dp = lax.axis_size("dp")
    n_mp = lax.axis_size("mp")
    section_pos = lax.axis_index("section")
    dp_pos = lax.axis_index("dp")
    mp_pos = lax.axis_index("mp")
    rows_enc = patches.shape[0]
    feat_width = w_merge_out.shape[1]
    own_width = feat_width // n_mp
    piece_width = own_width // n_section
    k_pair = K_PAIR
    slot_len = SLOT
    seq_len = n_dp * k_pair * slot_len
    owners_all = n_section * n_dp
    encoded = layer_norm(patches, ln_gain, ln_bias)
    hidden = jax.nn.gelu(
        jnp.dot(encoded, w_merge_in, preferred_element_type=jnp.float32) + b_merge_in,
        approximate=False,
    ).astype(jnp.bfloat16)
    partial_value = jnp.dot(hidden, w_merge_out, preferred_element_type=jnp.float32)
    my_sizes = lax.dynamic_slice_in_dim(image_sizes, dp_pos, 1, 0)
    my_place = lax.dynamic_slice_in_dim(placement, dp_pos, 1, 0)
    my_offsets = lax.dynamic_slice_in_dim(offsets, dp_pos, 1, 0)
    send_src, send_in = slot_layout(
        my_sizes,
        my_place,
        my_offsets,
        jnp.arange(owners_all, dtype=jnp.int32),
        k_pair,
        slot_len,
        rows_enc,
    )
    send_src = send_src.reshape(owners_all, k_pair * slot_len)
    send_in = send_in.reshape(owners_all, k_pair * slot_len)
    owner_here = jnp.reshape(section_pos * n_dp + dp_pos, (1,))
    recv_src, recv_in = slot_layout(
        image_sizes, placement, offsets, owner_here, k_pair, slot_len, rows_enc
    )
    recv_in = recv_in.reshape(seq_len)
    ordered = (
        partial_value.reshape(rows_enc, n_mp, n_section, piece_width)
        .transpose(0, 2, 1, 3)
        .reshape(rows_enc, feat_width)
    )
    summed = lax.psum_scatter(
        ordered.astype(jnp.bfloat16), ("section", "mp"), scatter_dimension=1, tiled=True
    ).astype(jnp.float32)
    bias_piece = lax.dynamic_slice_in_dim(
        b_merge_out, mp_pos * own_width + section_pos * piece_width, piece_width, 0
    )
    merged = (summed + bias_piece).astype(jnp.bfloat16)
    outgoing = jnp.where(send_in[..., None], merged[send_src], jnp.zeros((), jnp.bfloat16))
    arrived = lax.all_to_all(outgoing, ("section", "dp"), split_axis=0, concat_axis=0, tiled=True)
    image_part = (
        arrived.reshape(n_section, n_dp, k_pair * slot_len, piece_width)
        .transpose(1, 2, 0, 3)
        .reshape(seq_len, own_width)
    )
    stream = jnp.where(recv_in[:, None], image_part, text_rows.reshape(seq_len, own_width))
    is_first = section_pos == 0
    is_last = section_pos == n_section - 1
    turn_count = 2 * n_section - 1
    incoming = jnp.zeros_like(stream)
    feed_slot = stream
    drain_slot = jnp.zeros_like(stream)
    for turn_idx in range(turn_count):
        entry_rows = feed_slot
        current = jnp.where(is_first, entry_rows, incoming)
        full_rows = lax.all_gather(current, "mp", axis=1, tiled=True)
        values = full_rows.astype(jnp.float32)
        square = jnp.mean(values * values, axis=-1, keepdims=True)
        normed = (values * lax.rsqrt(square + 1e-06) * section_gain[0]).astype(jnp.bfloat16)
        update = jnp.dot(normed, section_weight[0], preferred_element_type=jnp.float32)
        result = (current.astype(jnp.float32) + update).astype(jnp.bfloat16)
        if turn_idx < turn_count - 1:
            incoming = passed_along(result, "section", 1)
        if turn_idx < n_section - 1:
            feed_slot = passed_along(feed_slot, "section", -1)
        if turn_idx >= n_section:
            drain_slot = passed_along(drain_slot, "section", -1)
        if turn_idx >= n_section - 1:
            drain_slot = jnp.where(is_last, result, drain_slot)
    return drain_slot.reshape(1, 1, seq_len, own_width)


def solution(mesh):
    in_specs = (
        P("dp", None),
        P(),
        P(),
        P(None, ("section", "mp")),
        P(("section", "mp")),
        P(("section", "mp"), None),
        P(),
        P("section", "dp", None, "mp"),
        P("section", None),
        P("section", None, "mp"),
        P(),
        P(),
        P(),
    )
    out_specs = P("section", "dp", None, "mp")
    return jax.shard_map(
        per_device, mesh=mesh, in_specs=in_specs, out_specs=out_specs, check_vma=False
    )
```

profile of v0, /device:TPU:1, one launch (start us, length us, event | category | flops | bytes accessed | tf_op | source)
XLA Modules:
  0.0 491.2 jit_solution(13765709935928243632)
XLA Ops:
  6.5 6.5 %reshape.382 = f32[256,4,1280]{2,1,0:T(4,128)} reshape(bf16[256,5120]{1,0:T(8,128)(2,1)} %param.13) | data formatting | bytes 7864320 | tf_op jit(solution)/shard_map/reshape | solution.py:34
  13.0 3.3 reduce_sum.130
  16.3 4.0 multiply_reduce_fusion
  20.3 0.7 mul.190
  21.1 3.2 copy.27
  24.3 0.7 sub.64
  25.1 3.2 copy.26
  28.4 11.2 %convolution_convert_fusion = bf16[256,8192]{1,0:T(8,128)(2,1)} fusion(bf16[160,8192]{1,0:T(8,128)(2,1)S(1)} %copy-done, bf16[5120,160]{0,1:T(8,128)(2,1)} %param.16, f32[256,5120]{1,0:T(8,128)} %bitcast.84, f32[256,5120]{1,0:T(8,128)} %bitcast.85, f32[5120]{0:T(1024)S(1)} %add.230, f32[5120]{0:T(1024)S(1)} %mul.194, bf16[256,5120]{1,0:T(8,128)(2,1)} %param.13, ...), kind=kOutput, calls=%fused_computation.15 | convolution fusion | flops 1103183872 | bytes 21602944 | tf_op jit(solution)/shard_map/dot_general | solution.py:75
  39.6 8.2 %convert_element_type.115 = bf16[256,8,4,256]{3,2,1,0:T(4,128)(2,1)} reshape(bf16[256,8192]{1,0:T(8,128)(2,1)} %convolution_convert_fusion) | data formatting | bytes 8388608 | tf_op jit(solution)/shard_map/convert_element_type | solution.py:101
  47.8 3.2 copy.23
  51.1 6.2 %copy.28 = bf16[32,8,32,256]{3,1,2,0:T(8,128)(2,1)} copy(bf16[32,8,32,256]{3,2,1,0:T(8,128)(2,1)S(1)} %bitcast.88) | data formatting | bytes 8388608
  59.1 0.8 dynamic_slice.15
  60.1 81.0 %reduce-scatter.2.cloned.1.call-done = bf16[256,256]{1,0:T(8,128)(2,1)} async-done(((bf16[256,8192]{1,0:T(8,128)(2,1)}), bf16[256,256]{1,0:T(8,128)(2,1)}) %reduce-scatter.2.cloned.1.call-update) | async-done | bytes 131088 | tf_op jit(solution)/shard_map/reduce_scatter | solution.py:100
  141.2 0.9 add_convert_fusion.10
  142.1 2.0 gather_fusion
  144.1 0.8 broadcast_select_fusion
  144.9 5.5 %all-to-all-start = ((bf16[16,32,256]{2,1,0:T(8,128)(2,1)}), bf16[16,32,256]{2,1,0:T(8,128)(2,1)S(1)}, u32[]{:S(2)}, u32[]{:S(2)}) async-start(bf16[16,32,256]{2,1,0:T(8,128)(2,1)} %broadcast_select_fusion), calls=%async_computation.1 | async-start | bytes 524288 | tf_op jit(solution)/shard_map/all_to_all | solution.py:108
  150.7 7.1 %all-to-all-done = bf16[16,32,256]{2,1,0:T(8,128)(2,1)S(1)} async-done(((bf16[16,32,256]{2,1,0:T(8,128)(2,1)}), bf16[16,32,256]{2,1,0:T(8,128)(2,1)S(1)}, u32[]{:S(2)}, u32[]{:S(2)}) %all-to-all-start) | async-done | bytes 262176 | tf_op jit(solution)/shard_map/all_to_all | solution.py:108
  158.0 0.8 broadcast_select_fusion.7
  158.9 1.3 collective-permute-start
  160.2 24.7 %all-gather.8.cloned.1.call-done = bf16[128,8192]{1,0:T(8,128)(2,1)} async-done(((bf16[128,1024]{1,0:T(8,128)(2,1)}), bf16[128,8192]{1,0:T(8,128)(2,1)}) %all-gather.8.cloned.1.call-update) | async-done | bytes 2097168 | tf_op jit(solution)/shard_map/all_gather | solution.py:124
  184.9 2.1 fusion.14
  187.0 8.7 %fusion.63 = bf16[128,1024]{1,0:T(8,128)(2,1)S(1)} fusion(bf16[1,8192,1024]{2,1,0:T(8,128)(2,1)} %param.22, bf16[128,8192]{1,0:T(8,128)(2,1)} %all-gather.8.cloned.1.call-done, f32[8192]{0:T(1024)S(1)} %bitcast.93, f32[128]{0:T(128)S(1)} %add_rsqrt_fusion.7, bf16[128,1024]{1,0:T(8,128)(2,1)} %get-tuple-element.16), kind=kOutput, calls=%fused_computation.70 | convolution fusion | flops 2152071168 | bytes 19431936 | tf_op jit(solution)/shard_map/dot_general | solution.py:128
  195.8 3.1 collective-permute-start.3
  198.9 5.4 %collective-permute-done.3 = bf16[128,1024]{1,0:T(8,128)(2,1)S(1)} collective-permute-done((bf16[128,1024]{1,0:T(8,128)(2,1)S(1)}, bf16[128,1024]{1,0:T(8,128)(2,1)S(1)}, u32[]{:S(2)}, u32[]{:S(2)}) %collective-permute-start.3) | collective-permute-done | bytes 262176 | tf_op jit(solution)/shard_map/ppermute | solution.py:13
  204.3 0.7 broadcast_select_fusion.6
  205.1 1.5 collective-permute-start.1
  206.6 26.2 %all-gather.10.cloned.1.call-done = bf16[128,8192]{1,0:T(8,128)(2,1)} async-done(((bf16[128,1024]{1,0:T(8,128)(2,1)}), bf16[128,8192]{1,0:T(8,128)(2,1)}) %all-gather.10.cloned.1.call-update) | async-done | bytes 2097168 | tf_op jit(solution)/shard_map/all_gather | solution.py:124
  232.8 2.1 fusion.17
  234.9 8.8 %add_convert_fusion.9 = bf16[128,1024]{1,0:T(8,128)(2,1)S(1)} fusion(bf16[128,1024]{1,0:T(8,128)(2,1)} %broadcast_select_fusion.6, bf16[1,8192,1024]{2,1,0:T(8,128)(2,1)} %param.22, bf16[128,8192]{1,0:T(8,128)(2,1)} %all-gather.10.cloned.1.call-done, f32[128]{0:T(128)S(1)} %add_rsqrt_fusion.6, f32[8192]{0:T(1024)S(1)} %bitcast.94), kind=kOutput, calls=%fused_computation.77 | convolution fusion | flops 2152071168 | bytes 19431936 | tf_op jit(solution)/shard_map/dot_general | solution.py:128
  243.6 3.1 collective-permute-start.4
  246.8 5.4 %collective-permute-done.4 = bf16[128,1024]{1,0:T(8,128)(2,1)S(1)} collective-permute-done((bf16[128,1024]{1,0:T(8,128)(2,1)S(1)}, bf16[128,1024]{1,0:T(8,128)(2,1)S(1)}, u32[]{:S(2)}, u32[]{:S(2)}) %collective-permute-start.4) | collective-permute-done | bytes 262176 | tf_op jit(solution)/shard_map/ppermute | solution.py:13
  252.2 0.7 broadcast_select_fusion.5
  253.0 1.3 collective-permute-start.2
  254.3 26.4 %all-gather.12.cloned.1.call-done = bf16[128,8192]{1,0:T(8,128)(2,1)} async-done(((bf16[128,1024]{1,0:T(8,128)(2,1)}), bf16[128,8192]{1,0:T(8,128)(2,1)}) %all-gather.12.cloned.1.call-update) | async-done | bytes 2097168 | tf_op jit(solution)/shard_map/all_gather | solution.py:124
  280.6 2.1 fusion.20
  282.7 8.8 %add_convert_fusion.8 = bf16[128,1024]{1,0:T(8,128)(2,1)S(1)} fusion(bf16[128,1024]{1,0:T(8,128)(2,1)} %broadcast_select_fusion.5, bf16[1,8192,1024]{2,1,0:T(8,128)(2,1)} %param.22, bf16[128,8192]{1,0:T(8,128)(2,1)} %all-gather.12.cloned.1.call-done, f32[128]{0:T(128)S(1)} %add_rsqrt_fusion.5, f32[8192]{0:T(1024)S(1)} %bitcast.95), kind=kOutput, calls=%fused_computation.76 | convolution fusion | flops 2152071168 | bytes 19431936 | tf_op jit(solution)/shard_map/dot_general | solution.py:128
  291.5 3.1 collective-permute-start.5
  294.6 5.4 %collective-permute-done.5 = bf16[128,1024]{1,0:T(8,128)(2,1)S(1)} collective-permute-done((bf16[128,1024]{1,0:T(8,128)(2,1)S(1)}, bf16[128,1024]{1,0:T(8,128)(2,1)S(1)}, u32[]{:S(2)}, u32[]{:S(2)}) %collective-permute-start.5) | collective-permute-done | bytes 262176 | tf_op jit(solution)/shard_map/ppermute | solution.py:13
  300.0 0.7 broadcast_select_fusion.4
  300.8 27.7 %all-gather.14.cloned.1.call-done = bf16[128,8192]{1,0:T(8,128)(2,1)} async-done(((bf16[128,1024]{1,0:T(8,128)(2,1)}), bf16[128,8192]{1,0:T(8,128)(2,1)}) %all-gather.14.cloned.1.call-update) | async-done | bytes 2097168 | tf_op jit(solution)/shard_map/all_gather | solution.py:124
  328.5 2.1 fusion.23
  330.6 8.8 %broadcast_select_fusion.10 = (bf16[128,1024]{1,0:T(8,128)(2,1)S(1)}, bf16[128,1024]{1,0:T(8,128)(2,1)S(1)}) fusion(pred[]{:T(512)S(6)} %eq.62, bf16[128,1024]{1,0:T(8,128)(2,1)} %broadcast_select_fusion.4, bf16[1,8192,1024]{2,1,0:T(8,128)(2,1)} %param.22, bf16[128,8192]{1,0:T(8,128)(2,1)} %all-gather.14.cloned.1.call-done, f32[128]{0:T(128)S(1)} %add_rsqrt_fusion.4, ...), kind=kOutput, calls=%fused_computation.92 | convolution fusion | flops 2152202240 | bytes 19694080 | tf_op jit(solution)/shard_map/dot_general | solution.py:128
  339.4 3.1 collective-permute-start.6
  342.5 5.4 %collective-permute-done.6 = bf16[128,1024]{1,0:T(8,128)(2,1)S(1)} collective-permute-done((bf16[128,1024]{1,0:T(8,128)(2,1)S(1)}, bf16[128,1024]{1,0:T(8,128)(2,1)S(1)}, u32[]{:S(2)}, u32[]{:S(2)}) %collective-permute-start.6) | collective-permute-done | bytes 262176 | tf_op jit(solution)/shard_map/ppermute | solution.py:13
  347.9 0.7 broadcast_select_fusion.3
  348.7 1.5 collective-permute-start.9
  350.2 26.2 %all-gather.16.cloned.1.call-done = bf16[128,8192]{1,0:T(8,128)(2,1)} async-done(((bf16[128,1024]{1,0:T(8,128)(2,1)}), bf16[128,8192]{1,0:T(8,128)(2,1)}) %all-gather.16.cloned.1.call-update) | async-done | bytes 2097168 | tf_op jit(solution)/shard_map/all_gather | solution.py:124
  376.4 2.1 fusion.26
  378.5 8.8 %fusion.4 = f32[128,1024]{1,0:T(8,128)S(1)} fusion(bf16[1,8192,1024]{2,1,0:T(8,128)(2,1)} %param.22, bf16[128,8192]{1,0:T(8,128)(2,1)} %all-gather.16.cloned.1.call-done, f32[128]{0:T(128)S(1)} %add_rsqrt_fusion.3, f32[8192]{0:T(1024)S(1)} %bitcast.97), kind=kOutput, calls=%fused_computation.5 | convolution fusion | flops 2151677952 | bytes 19431936 | tf_op jit(solution)/shard_map/dot_general | solution.py:128
  387.5 3.1 collective-permute-start.7
  390.6 5.4 %collective-permute-done.7 = bf16[128,1024]{1,0:T(8,128)(2,1)S(1)} collective-permute-done((bf16[128,1024]{1,0:T(8,128)(2,1)S(1)}, bf16[128,1024]{1,0:T(8,128)(2,1)S(1)}, u32[]{:S(2)}, u32[]{:S(2)}) %collective-permute-start.7) | collective-permute-done | bytes 262176 | tf_op jit(solution)/shard_map/ppermute | solution.py:13
  396.0 0.7 broadcast_select_fusion.2
  396.8 1.3 collective-permute-start.10
  398.1 26.4 %all-gather.18.cloned.1.call-done = bf16[128,8192]{1,0:T(8,128)(2,1)} async-done(((bf16[128,1024]{1,0:T(8,128)(2,1)}), bf16[128,8192]{1,0:T(8,128)(2,1)}) %all-gather.18.cloned.1.call-update) | async-done | bytes 2097168 | tf_op jit(solution)/shard_map/all_gather | solution.py:124
  424.5 2.1 fusion.29
  426.6 8.8 %broadcast_select_fusion.8 = (bf16[128,1024]{1,0:T(8,128)(2,1)S(1)}, bf16[128,1024]{1,0:T(8,128)(2,1)S(1)}) fusion(bf16[128,1024]{1,0:T(8,128)(2,1)S(1)} %collective-permute-done.10, pred[]{:T(512)S(6)} %eq.62, bf16[128,1024]{1,0:T(8,128)(2,1)} %broadcast_select_fusion.2, bf16[1,8192,1024]{2,1,0:T(8,128)(2,1)} %param.22, ...), kind=kOutput, calls=%fused_computation.90 | convolution fusion | flops 2152202240 | bytes 19956224 | tf_op jit(solution)/shard_map/dot_general | solution.py:128
  435.4 3.1 collective-permute-start.8
  438.5 5.4 %collective-permute-done.8 = bf16[128,1024]{1,0:T(8,128)(2,1)S(1)} collective-permute-done((bf16[128,1024]{1,0:T(8,128)(2,1)S(1)}, bf16[128,1024]{1,0:T(8,128)(2,1)S(1)}, u32[]{:S(2)}, u32[]{:S(2)}) %collective-permute-start.8) | collective-permute-done | bytes 262176 | tf_op jit(solution)/shard_map/ppermute | solution.py:13
  443.9 0.7 broadcast_select_fusion.1
  444.7 1.3 collective-permute-start.11
  446.0 26.4 %all-gather.20.cloned.1.call-done = bf16[128,8192]{1,0:T(8,128)(2,1)} async-done(((bf16[128,1024]{1,0:T(8,128)(2,1)}), bf16[128,8192]{1,0:T(8,128)(2,1)}) %all-gather.20.cloned.1.call-update) | async-done | bytes 2097168 | tf_op jit(solution)/shard_map/all_gather | solution.py:124
  472.4 2.1 fusion.32
  474.5 9.6 %fusion.70 = bf16[1,1,128,1024]{3,2,1,0:T(8,128)(2,1)} fusion(bf16[128,1024]{1,0:T(8,128)(2,1)S(1)} %collective-permute-done.11, bf16[128,1024]{1,0:T(8,128)(2,1)} %broadcast_select_fusion.1, pred[]{:T(512)S(6)} %eq.62, bf16[1,8192,1024]{2,1,0:T(8,128)(2,1)} %param.22, bf16[128,8192]{1,0:T(8,128)(2,1)} %all-gather.20.cloned.1.call-done, ...), kind=kOutput, calls=%fused_computation.79 | convolution fusion | flops 2152202240 | bytes 19694080 | tf_op jit(solution)/shard_map/dot_general | solution.py:128
  (82 shorter events, 3.1 us)
Async XLA Ops:
  6.5 21.8 %copy-start = (bf16[160,8192]{1,0:T(8,128)(2,1)S(1)}, bf16[160,8192]{1,0:T(8,128)(2,1)}, u32[]{:S(2)}) copy-start(bf16[160,8192]{1,0:T(8,128)(2,1)} %param.18) | copy-start | bytes 7864324
  6.5 134.6 %reduce-scatter.2.cloned.1.call-start = ((), (), s32[]{:S(2)}) async-start(), calls=%async_computation.2 | async-start | bytes 4325376 | tf_op jit(solution)/shard_map/reduce_scatter | solution.py:100
  25.0 3.3 copy-start.4
  25.0 3.3 copy-start.5
  25.1 3.3 copy-start.6
  57.3 0.7 copy-start.9
  57.3 0.9 copy-start.7
  57.3 0.9 copy-start.8
  57.3 100.7 %copy-start.3 = (bf16[1,1,128,1024]{3,2,1,0:T(8,128)(2,1)S(1)}, bf16[1,1,128,1024]{3,2,1,0:T(8,128)(2,1)}, u32[]{:S(2)}) copy-start(bf16[1,1,128,1024]{3,2,1,0:T(8,128)(2,1)} %param.20) | copy-start | bytes 786436
  57.3 129.7 %copy-start.10 = (f32[1,8192]{1,0:T(1,128)S(1)}, f32[1,8192]{1,0:T(1,128)}, u32[]{:S(2)}) copy-start(f32[1,8192]{1,0:T(1,128)} %param.21) | copy-start | bytes 98308
  144.9 12.8 %all-to-all-start = ((bf16[16,32,256]{2,1,0:T(8,128)(2,1)}), bf16[16,32,256]{2,1,0:T(8,128)(2,1)S(1)}, u32[]{:S(2)}, u32[]{:S(2)}) async-start(bf16[16,32,256]{2,1,0:T(8,128)(2,1)} %broadcast_select_fusion), calls=%async_computation.1 | async-start | bytes 524288 | tf_op jit(solution)/shard_map/all_to_all | solution.py:108
  150.4 34.5 %all-gather.8.cloned.1.call-start = ((), (), s32[]{:S(2)}) async-start(), calls=%async_computation.3 | async-start | bytes 2359296 | tf_op jit(solution)/shard_map/all_gather | solution.py:124
  158.8 73.9 %all-gather.10.cloned.1.call-start = ((), (), s32[]{:S(2)}) async-start(), calls=%async_computation.4 | async-start | bytes 2359296 | tf_op jit(solution)/shard_map/all_gather | solution.py:124
  158.9 40.0 %collective-permute-start = (bf16[128,1024]{1,0:T(8,128)(2,1)S(1)}, bf16[128,1024]{1,0:T(8,128)(2,1)S(1)}, u32[]{:S(2)}, u32[]{:S(2)}) collective-permute-start(bf16[128,1024]{1,0:T(8,128)(2,1)S(1)} %get-tuple-element.17), channel_id=1, source_target_pairs={{32,0},{64,32},{96,64},{33,1},{65,33},{97,65},{34,2},{66,34},{98,6... | collective-permute-start | bytes 786440 | tf_op jit(solution)/shard_map/ppermute | solution.py:13
  195.8 8.6 %collective-permute-start.3 = (bf16[128,1024]{1,0:T(8,128)(2,1)S(1)}, bf16[128,1024]{1,0:T(8,128)(2,1)S(1)}, u32[]{:S(2)}, u32[]{:S(2)}) collective-permute-start(bf16[128,1024]{1,0:T(8,128)(2,1)S(1)} %fusion.63), channel_id=1, source_target_pairs={{0,32},{32,64},{64,96},{1,33},{33,65},{65,97},{2,34},{34,66},{66,9... | collective-permute-start | bytes 786440 | tf_op jit(solution)/shard_map/ppermute | solution.py:13
  205.1 75.6 %all-gather.12.cloned.1.call-start = ((), (), s32[]{:S(2)}) async-start(), calls=%async_computation.5 | async-start | bytes 2359296 | tf_op jit(solution)/shard_map/all_gather | solution.py:124
  205.1 41.6 %collective-permute-start.1 = (bf16[128,1024]{1,0:T(8,128)(2,1)S(1)}, bf16[128,1024]{1,0:T(8,128)(2,1)S(1)}, u32[]{:S(2)}, u32[]{:S(2)}) collective-permute-start(bf16[128,1024]{1,0:T(8,128)(2,1)S(1)} %collective-permute-done), channel_id=1, source_target_pairs={{32,0},{64,32},{96,64},{33,1},{65,33},{97,65},{34,2},{66,34},{98,6... | collective-permute-start | bytes 786440 | tf_op jit(solution)/shard_map/ppermute | solution.py:13
  243.6 8.5 %collective-permute-start.4 = (bf16[128,1024]{1,0:T(8,128)(2,1)S(1)}, bf16[128,1024]{1,0:T(8,128)(2,1)S(1)}, u32[]{:S(2)}, u32[]{:S(2)}) collective-permute-start(bf16[128,1024]{1,0:T(8,128)(2,1)S(1)} %add_convert_fusion.9), channel_id=1, source_target_pairs={{0,32},{32,64},{64,96},{1,33},{33,65},{65,97},{2,34},{34,66},{66,9... | collective-permute-start | bytes 786440 | tf_op jit(solution)/shard_map/ppermute | solution.py:13
  252.9 75.6 %all-gather.14.cloned.1.call-start = ((), (), s32[]{:S(2)}) async-start(), calls=%async_computation.6 | async-start | bytes 2359296 | tf_op jit(solution)/shard_map/all_gather | solution.py:124
  253.0 41.6 %collective-permute-start.2 = (bf16[128,1024]{1,0:T(8,128)(2,1)S(1)}, bf16[128,1024]{1,0:T(8,128)(2,1)S(1)}, u32[]{:S(2)}, u32[]{:S(2)}) collective-permute-start(bf16[128,1024]{1,0:T(8,128)(2,1)S(1)} %collective-permute-done.1), channel_id=1, source_target_pairs={{32,0},{64,32},{96,64},{33,1},{65,33},{97,65},{34,2},{66,34},{98,6... | collective-permute-start | bytes 786440 | tf_op jit(solution)/shard_map/ppermute | solution.py:13
  291.5 8.5 %collective-permute-start.5 = (bf16[128,1024]{1,0:T(8,128)(2,1)S(1)}, bf16[128,1024]{1,0:T(8,128)(2,1)S(1)}, u32[]{:S(2)}, u32[]{:S(2)}) collective-permute-start(bf16[128,1024]{1,0:T(8,128)(2,1)S(1)} %add_convert_fusion.8), channel_id=1, source_target_pairs={{0,32},{32,64},{64,96},{1,33},{33,65},{65,97},{2,34},{34,66},{66,9... | collective-permute-start | bytes 786440 | tf_op jit(solution)/shard_map/ppermute | solution.py:13
  300.8 75.6 %all-gather.16.cloned.1.call-start = ((), (), s32[]{:S(2)}) async-start(), calls=%async_computation.7 | async-start | bytes 2359296 | tf_op jit(solution)/shard_map/all_gather | solution.py:124
  339.4 8.5 %collective-permute-start.6 = (bf16[128,1024]{1,0:T(8,128)(2,1)S(1)}, bf16[128,1024]{1,0:T(8,128)(2,1)S(1)}, u32[]{:S(2)}, u32[]{:S(2)}) collective-permute-start(bf16[128,1024]{1,0:T(8,128)(2,1)S(1)} %get-tuple-element.15), channel_id=1, source_target_pairs={{0,32},{32,64},{64,96},{1,33},{33,65},{65,97},{2,34},{34,66},{66,9... | collective-permute-start | bytes 786440 | tf_op jit(solution)/shard_map/ppermute | solution.py:13
  348.7 75.8 %all-gather.18.cloned.1.call-start = ((), (), s32[]{:S(2)}) async-start(), calls=%async_computation.8 | async-start | bytes 2359296 | tf_op jit(solution)/shard_map/all_gather | solution.py:124
  348.7 38.6 %collective-permute-start.9 = (bf16[128,1024]{1,0:T(8,128)(2,1)S(1)}, bf16[128,1024]{1,0:T(8,128)(2,1)S(1)}, u32[]{:S(2)}, u32[]{:S(2)}) collective-permute-start(bf16[128,1024]{1,0:T(8,128)(2,1)S(1)} %get-tuple-element.14), channel_id=1, source_target_pairs={{32,0},{64,32},{96,64},{33,1},{65,33},{97,65},{34,2},{66,34},{98,6... | collective-permute-start | bytes 786440 | tf_op jit(solution)/shard_map/ppermute | solution.py:13
  378.5 8.8 %copy-start.2 = (bf16[128,1024]{1,0:T(8,128)(2,1)S(1)}, bf16[128,1024]{1,0:T(8,128)(2,1)}, u32[]{:S(2)}) copy-start(bf16[128,1024]{1,0:T(8,128)(2,1)} %broadcast_select_fusion.3) | copy-start | bytes 786436
  387.5 8.5 %collective-permute-start.7 = (bf16[128,1024]{1,0:T(8,128)(2,1)S(1)}, bf16[128,1024]{1,0:T(8,128)(2,1)S(1)}, u32[]{:S(2)}, u32[]{:S(2)}) collective-permute-start(bf16[128,1024]{1,0:T(8,128)(2,1)S(1)} %get-tuple-element.13), channel_id=1, source_target_pairs={{0,32},{32,64},{64,96},{1,33},{33,65},{65,97},{2,34},{34,66},{66,9... | collective-permute-start | bytes 786440 | tf_op jit(solution)/shard_map/ppermute | solution.py:13
  396.8 75.6 %all-gather.20.cloned.1.call-start = ((), (), s32[]{:S(2)}) async-start(), calls=%async_computation.9 | async-start | bytes 2359296 | tf_op jit(solution)/shard_map/all_gather | solution.py:124
  396.8 29.8 %collective-permute-start.10 = (bf16[128,1024]{1,0:T(8,128)(2,1)S(1)}, bf16[128,1024]{1,0:T(8,128)(2,1)S(1)}, u32[]{:S(2)}, u32[]{:S(2)}) collective-permute-start(bf16[128,1024]{1,0:T(8,128)(2,1)S(1)} %get-tuple-element.12), channel_id=1, source_target_pairs={{32,0},{64,32},{96,64},{33,1},{65,33},{97,65},{34,2},{66,34},{98,6... | collective-permute-start | bytes 786440 | tf_op jit(solution)/shard_map/ppermute | solution.py:13
  435.4 8.5 %collective-permute-start.8 = (bf16[128,1024]{1,0:T(8,128)(2,1)S(1)}, bf16[128,1024]{1,0:T(8,128)(2,1)S(1)}, u32[]{:S(2)}, u32[]{:S(2)}) collective-permute-start(bf16[128,1024]{1,0:T(8,128)(2,1)S(1)} %get-tuple-element.11), channel_id=1, source_target_pairs={{0,32},{32,64},{64,96},{1,33},{33,65},{65,97},{2,34},{34,66},{66,9... | collective-permute-start | bytes 786440 | tf_op jit(solution)/shard_map/ppermute | solution.py:13
  444.7 29.8 %collective-permute-start.11 = (bf16[128,1024]{1,0:T(8,128)(2,1)S(1)}, bf16[128,1024]{1,0:T(8,128)(2,1)S(1)}, u32[]{:S(2)}, u32[]{:S(2)}) collective-permute-start(bf16[128,1024]{1,0:T(8,128)(2,1)S(1)} %get-tuple-element.10), channel_id=1, source_target_pairs={{32,0},{64,32},{96,64},{33,1},{65,33},{97,65},{34,2},{66,34},{98,6... | collective-permute-start | bytes 786440 | tf_op jit(solution)/shard_map/ppermute | solution.py:13
  474.5 9.7 %copy-start.1 = (bf16[160,8192]{1,0:T(8,128)(2,1)S(1)}, bf16[160,8192]{1,0:T(8,128)(2,1)}, u32[]{:S(2)}) copy-start(bf16[160,8192]{1,0:T(8,128)(2,1)} %param.18) | copy-start | bytes 7864324
Sparse Core Ops, SparseCore 0:
  57.5 83.6 reduce-scatter.1
  159.0 25.9 all-gather.7
  205.2 27.5 all-gather.9
  253.0 27.5 all-gather.11
  300.9 27.5 all-gather.13
  348.8 27.5 all-gather.15
  396.9 27.5 all-gather.17
  444.8 27.5 all-gather.19
where the time goes:
time: 500 us; the launch traced here: 491 us
  waiting for transfers between devices  305 us (61%)
  matrix products  73.5 us (15%)
  local copies, waits for them, and re-layouts  36.1 us (7%)
  starting transfers between devices  32.6 us (7%)
  other arithmetic  30.2 us (6%)
  between operations  14.2 us (3%)
    all_gather x7, waiting for transfers between devices, per_device(): full_rows = lax.all_gather(current, 'mp', axis=1, tiled=True)  184 us
    reduce_scatter x1, waiting for transfers between devices, per_device(): lax.psum_scatter(ordered.astype(jnp.bfloat16), ('section', 'mp'), scatter...  81 us
    dot_general x7, matrix products, per_device(): jnp.dot(normed, section_weight[0], preferred_element_type=jnp.float32)  62.3 us
    ppermute x12, waiting for transfers between devices, passed_along(): return lax.ppermute(block, axis, route)  32.5 us
    ppermute x12, starting transfers between devices, passed_along(): return lax.ppermute(block, axis, route)  26.8 us
    reduce_sum x7, other arithmetic, per_device(): square = jnp.mean(values * values, axis=-1, keepdims=True)  14.5 us
    unnamed x26, local copies, waits for them, and re-layouts  13.3 us
    convert_element_type x2, local copies, waits for them, and re-layouts, per_device(): ordered.astype(jnp.bfloat16)  11.5 us
  transfers between devices with their start and end apart: 21, of which 15 were waited for; matrix products, arithmetic and copies ran while one was open for 10% of the time, Pallas kernels for 0%

commit v1 on v0

--- a/solution.py
+++ b/solution.py
@@ -1,22 +1,22 @@
 import jax
 import jax.numpy as jnp
 from jax import lax
+from jax.experimental import pallas as pl
+from jax.experimental.pallas import tpu as pltpu
 from jax.sharding import PartitionSpec as P
 
 SLOT = 8
 K_PAIR = 4
-
-
-def passed_along(block, axis, distance):
-    devices = range(lax.axis_size(axis))
-    route = [(i - distance, i) for i in devices if i - distance in devices]
-    return lax.ppermute(block, axis, route)
+ROWS = 64
+MESH = pl.DeviceIdType.MESH
 
 
 def slot_layout(image_sizes, placement, offsets, owners, k_pair, slot_len, rows_enc):
     targets = owners[:, None] * k_pair + jnp.arange(k_pair, dtype=jnp.int32)[None, :]
     matches = placement[:, None, None, :] == targets[None, :, :, None]
-    starts = jnp.cumsum(image_sizes, axis=1) - image_sizes
+    count = image_sizes.shape[1]
+    earlier = jnp.arange(count)[:, None] < jnp.arange(count)[None, :]
+    starts = jnp.sum(jnp.where(earlier[None], image_sizes[:, :, None], 0), axis=1)
 
     def picker(values):
         return jnp.sum(jnp.where(matches, values[:, None, None, :], 0), axis=-1)
@@ -36,6 +36,217 @@
     spread = jnp.mean(centre * centre, axis=-1, keepdims=True)
     normed = centre * lax.rsqrt(spread + 1e-06) * ln_gain + ln_bias
     return normed.reshape(patches.shape[0], -1).astype(jnp.bfloat16)
+
+
+def layers_kernel(
+    stream_ref, gain_ref, weight_hbm, out_ref,
+    shards, weight, total, squares, results,
+    weight_sem, got, sent, home_sem, gone_sem,
+):
+    section = lax.axis_index("section")
+    mp = lax.axis_index("mp")
+    n_section = lax.axis_size("section")
+    n_mp = lax.axis_size("mp")
+    n_ring = n_mp // 2
+    chip, core = mp // 2, lax.rem(mp, 2)
+    chunks, _, rows, width = shards.shape
+    per_micro = chunks // n_section
+
+    def at(chip_pos, core_pos):
+        return lax.rem(chip_pos + n_ring, n_ring) * 2 + core_pos
+
+    ahead, behind = at(chip + 1, core), at(chip - 1, core)
+    sibling = at(chip, 1 - core)
+    turn = 1 - 2 * core
+    onward, source = at(chip + turn, core), at(chip - turn, core)
+    far = at(chip + 2, core)
+
+    def shard_copy(t, idx, slot, **target):
+        return pltpu.make_async_remote_copy(
+            src_ref=shards.at[t, idx], dst_ref=shards.at[t, idx],
+            send_sem=sent.at[t, slot], recv_sem=got.at[t, idx],
+            device_id=target, device_id_type=MESH,
+        )
+
+    def arrival(t, idx):
+        shard_copy(t, idx, 0, mp=sibling).wait_recv()
+
+    def load(idx):
+        return pltpu.make_async_copy(weight_hbm.at[idx], weight.at[idx], weight_sem.at[idx])
+
+    for idx in range(n_mp):
+        load(idx).start()
+
+    barrier = pltpu.get_barrier_semaphore()
+    for partner in (ahead, behind, sibling):
+        pl.semaphore_signal(barrier, inc=1, device_id={"mp": partner}, device_id_type=MESH)
+    for hop in range(1, n_section):
+        pl.semaphore_signal(
+            barrier, inc=1, device_id={"section": lax.rem(section + hop, n_section)}, device_id_type=MESH
+        )
+    pl.semaphore_wait(barrier, 2 + n_section)
+
+    def feed(half, t):
+        return pltpu.make_async_remote_copy(
+            src_ref=stream_ref.at[pl.ds(half * rows, rows)], dst_ref=shards.at[t, mp],
+            send_sem=gone_sem.at[half], recv_sem=got.at[t, mp],
+            device_id={"section": 0}, device_id_type=MESH,
+        )
+
+    for half in range(per_micro):
+        @pl.when(section == 0)
+        def _():
+            pltpu.make_async_copy(
+                stream_ref.at[pl.ds(half * rows, rows)], shards.at[half, mp], got.at[half, mp]
+            ).start()
+
+        @pl.when(section != 0)
+        def _():
+            feed(half, section * per_micro + half).start()
+
+    def pass_on(t):
+        return pltpu.make_async_remote_copy(
+            src_ref=results.at[t], dst_ref=shards.at[t, mp],
+            send_sem=sent.at[t, 7], recv_sem=got.at[t, mp],
+            device_id={"section": section + 1}, device_id_type=MESH,
+        )
+
+    def bring_home(t):
+        half = lax.rem(t, per_micro)
+        return pltpu.make_async_remote_copy(
+            src_ref=results.at[t], dst_ref=out_ref.at[pl.ds(pl.multiple_of(half * rows, rows), rows)],
+            send_sem=sent.at[t, 7], recv_sem=home_sem.at[half],
+            device_id={"section": t // per_micro}, device_id_type=MESH,
+        )
+
+    def add(t, idx):
+        values = shards[t, idx].astype(jnp.float32)
+        square = values * values
+        lanes = squares[...]
+        for j in range(0, width, 128):
+            lanes = lanes + square[:, j : j + 128]
+        squares[...] = lanes
+        scaled = (values * gain_ref[pl.ds(idx, 1), :]).astype(jnp.bfloat16)
+        total[...] += jnp.dot(scaled, weight[idx], preferred_element_type=jnp.float32)
+
+    last = n_section - 1
+
+    def turn_body(i, carry):
+        t = i - 1
+
+        @pl.when(i < chunks)
+        def _():
+            arrival(i, mp)
+            shard_copy(i, mp, 0, mp=onward).start()
+            shard_copy(i, mp, 1, mp=source).start()
+            shard_copy(i, mp, 2, mp=sibling).start()
+
+        @pl.when(i == 1)
+        def _():
+            for idx in range(n_mp):
+                load(idx).wait()
+
+        @pl.when(i > 0)
+        def _():
+            total[...] = jnp.zeros_like(total)
+            squares[...] = jnp.zeros_like(squares)
+            add(t, mp)
+            add(t, source)
+            add(t, onward)
+            arrival(t, far)
+            shard_copy(t, far, 3, mp=sibling).start()
+            add(t, far)
+            for step in (0, 1, -1):
+                idx = at(chip + step, 1 - core)
+                arrival(t, idx)
+                add(t, idx)
+
+        @pl.when(i < chunks)
+        def _():
+            arrival(i, source)
+            shard_copy(i, source, 4, mp=onward).start()
+            shard_copy(i, source, 5, mp=sibling).start()
+            arrival(i, onward)
+            shard_copy(i, onward, 6, mp=sibling).start()
+
+        @pl.when(i > 0)
+        def _():
+            idx = at(chip + 2, 1 - core)
+            arrival(t, idx)
+            add(t, idx)
+            square = jnp.sum(squares[...], axis=-1, keepdims=True) * (1.0 / (n_mp * width))
+            update = total[...] * lax.rsqrt(square + 1e-06)
+            result = (shards[t, mp].astype(jnp.float32) + update).astype(jnp.bfloat16)
+            results[t] = result
+
+            @pl.when(section < last)
+            def _():
+                pass_on(t).start()
+
+            @pl.when((section == last) & (t < last * per_micro))
+            def _():
+                bring_home(t).start()
+
+            @pl.when((section == last) & (t >= last * per_micro))
+            def _():
+                half = lax.rem(t, per_micro)
+                out_ref[pl.ds(pl.multiple_of(half * rows, rows), rows)] = result
+
+        return carry
+
+    lax.fori_loop(0, chunks + 1, turn_body, 0)
+
+    @pl.when(section < last)
+    def _():
+        for half in range(per_micro):
+            bring_home(half).wait_recv()
+
+    def settle(t, carry):
+        for slot in range(7):
+            shard_copy(t, mp, slot, mp=sibling).wait_send()
+
+        @pl.when((section < last) | (t < last * per_micro))
+        def _():
+            shard_copy(t, mp, 7, mp=sibling).wait_send()
+
+        return carry
+
+    lax.fori_loop(0, chunks, settle, 0)
+
+    @pl.when(section != 0)
+    def _():
+        for half in range(per_micro):
+            feed(half, half).wait_send()
+
+
+def layers(stream, gain, weight, n_section, n_mp):
+    seq_len, width = stream.shape
+    chunks = n_section * seq_len // ROWS
+    return pl.pallas_call(
+        layers_kernel,
+        out_shape=jax.ShapeDtypeStruct((seq_len, width), jnp.bfloat16),
+        in_specs=[
+            pl.BlockSpec(memory_space=pltpu.VMEM),
+            pl.BlockSpec(memory_space=pltpu.VMEM),
+            pl.BlockSpec(memory_space=pl.ANY),
+        ],
+        out_specs=pl.BlockSpec(memory_space=pltpu.VMEM),
+        scratch_shapes=[
+            pltpu.VMEM((chunks, n_mp, ROWS, width), jnp.bfloat16),
+            pltpu.VMEM((n_mp, width, width), jnp.bfloat16),
+            pltpu.VMEM((ROWS, width), jnp.float32),
+            pltpu.VMEM((ROWS, 128), jnp.float32),
+            pltpu.VMEM((chunks, ROWS, width), jnp.bfloat16),
+            pltpu.SemaphoreType.DMA((n_mp,)),
+            pltpu.SemaphoreType.DMA((chunks, n_mp)),
+            pltpu.SemaphoreType.DMA((chunks, 8)),
+            pltpu.SemaphoreType.DMA((seq_len // ROWS,)),
+            pltpu.SemaphoreType.DMA((seq_len // ROWS,)),
+        ],
+        compiler_params=pltpu.CompilerParams(
+            collective_id=0, has_side_effects=True, vmem_limit_bytes=56 * 2**20
+        ),
+    )(stream, gain.reshape(n_mp, width), weight.reshape(n_mp, width, width))
 
 
 def per_device(
@@ -112,30 +323,8 @@
         .reshape(seq_len, own_width)
     )
     stream = jnp.where(recv_in[:, None], image_part, text_rows.reshape(seq_len, own_width))
-    is_first = section_pos == 0
-    is_last = section_pos == n_section - 1
-    turn_count = 2 * n_section - 1
-    incoming = jnp.zeros_like(stream)
-    feed_slot = stream
-    drain_slot = jnp.zeros_like(stream)
-    for turn_idx in range(turn_count):
-        entry_rows = feed_slot
-        current = jnp.where(is_first, entry_rows, incoming)
-        full_rows = lax.all_gather(current, "mp", axis=1, tiled=True)
-        values = full_rows.astype(jnp.float32)
-        square = jnp.mean(values * values, axis=-1, keepdims=True)
-        normed = (values * lax.rsqrt(square + 1e-06) * section_gain[0]).astype(jnp.bfloat16)
-        update = jnp.dot(normed, section_weight[0], preferred_element_type=jnp.float32)
-        result = (current.astype(jnp.float32) + update).astype(jnp.bfloat16)
-        if turn_idx < turn_count - 1:
-            incoming = passed_along(result, "section", 1)
-        if turn_idx < n_section - 1:
-            feed_slot = passed_along(feed_slot, "section", -1)
-        if turn_idx >= n_section:
-            drain_slot = passed_along(drain_slot, "section", -1)
-        if turn_idx >= n_section - 1:
-            drain_slot = jnp.where(is_last, result, drain_slot)
-    return drain_slot.reshape(1, 1, seq_len, own_width)
+    result = layers(stream, section_gain, section_weight, n_section, n_mp)
+    return result.reshape(1, 1, seq_len, own_width)
 
 
 def solution(mesh):

time: 500 us -> 281 us (0.56)
  the two profiles are of different devices: /device:TPU:1 before, /device:TPU:31 now
where the time goes in v1:
time: 281 us; the launch traced here: 278 us
  Pallas kernels  116 us (41%)
  waiting for transfers between devices  81.1 us (29%)
  local copies, waits for them, and re-layouts  38.1 us (14%)
  between operations  13.6 us (5%)
  other arithmetic  11.6 us (4%)
  matrix products  11.2 us (4%)
  starting transfers between devices  6.63 us (2%)
    pallas_call x1, Pallas kernels, layers(): pl.pallas_call(layers_kernel, out_shape=jax.ShapeDtypeStruct((seq_len, wi...  116 us
    reduce_scatter x1, waiting for transfers between devices, per_device(): lax.psum_scatter(ordered.astype(jnp.bfloat16), ('section', 'mp'), scatter...  79.6 us
    unnamed x26, local copies, waits for them, and re-layouts  15.1 us
    dot_general x1, matrix products, per_device(): jnp.dot(hidden, w_merge_out, preferred_element_type=jnp.float32)  11.2 us
    convert_element_type x2, local copies, waits for them, and re-layouts, per_device(): ordered.astype(jnp.bfloat16)  11 us
    all_to_all x1, starting transfers between devices, per_device(): lax.all_to_all(outgoing, ('section', 'dp'), split_axis=0, concat_axis=0,...  6.62 us
    reshape x1, local copies, waits for them, and re-layouts, layer_norm(): values = patches.astype(jnp.float32).reshape(patches.shape[0], 4, -1)  6.48 us
  transfers between devices with their start and end apart: 2, of which 2 were waited for; matrix products, arithmetic and copies ran while one was open for 2% of the time, Pallas kernels for 0%

profile of v1, /device:TPU:31, one launch (start us, length us, event | category | flops | bytes accessed | tf_op | source)
XLA Modules:
  0.0 277.9 jit_solution(7801468733837613823)
XLA Ops:
  6.5 0.0 copy-start
  6.5 0.0 reduce-scatter.2.cloned.1.call-start
  6.5 6.5 %reshape.381 = f32[256,4,1280]{2,1,0:T(4,128)} reshape(bf16[256,5120]{1,0:T(8,128)(2,1)} %param.13) | data formatting | bytes 7864320 | tf_op jit(solution)/shard_map/reshape | solution.py:34
  13.0 3.3 %reduce_sum.76 = f32[256,4]{1,0:T(8,128)S(1)} reduce(f32[256,4,1280]{2,1,0:T(4,128)} %reshape.381, f32[]{:T(128)} %constant.48.clone.1), dimensions={2}, to_apply=%region_4.5 | reduce | flops 1309696 | bytes 5246980 | tf_op jit(solution)/shard_map/reduce_sum | solution.py:35
  16.3 4.0 %multiply_reduce_fusion = f32[256,4]{1,0:T(8,128)S(1)} fusion(f32[256,4,1280]{2,1,0:T(4,128)} %reshape.381, f32[256,4]{1,0:T(8,128)S(1)} %broadcast_multiply_fusion), kind=kLoop, calls=%fused_computation.3 | loop fusion | flops 3931136 | bytes 5251072 | tf_op jit(solution)/shard_map/reduce_sum | solution.py:36
  20.3 0.7 mul.67
  21.1 3.2 %copy.27 = f32[32,8,4,1280]{3,1,2,0:T(8,128)} copy(f32[32,8,4,1280]{3,2,1,0:T(4,128)S(1)} %bitcast.49) | data formatting | bytes 10485760
  24.3 0.7 sub.61
  25.1 0.0 copy-start.4
  25.1 0.0 copy-start.5
  25.1 0.0 copy-start.6
  25.1 3.3 %copy.26 = f32[32,8,4,1280]{3,1,2,0:T(8,128)} copy(f32[32,8,4,1280]{3,2,1,0:T(4,128)S(1)} %bitcast.50) | data formatting | bytes 10485760
  28.4 0.0 copy-done.4
  28.4 0.0 copy-done.5
  28.4 0.0 copy-done
  28.4 0.0 copy-done.6
  28.4 11.2 %convolution_convert_fusion = bf16[256,8192]{1,0:T(8,128)(2,1)} fusion(bf16[160,8192]{1,0:T(8,128)(2,1)S(1)} %copy-done, bf16[5120,160]{0,1:T(8,128)(2,1)} %param.16, f32[256,5120]{1,0:T(8,128)} %bitcast.51, f32[256,5120]{1,0:T(8,128)} %bitcast.52, f32[5120]{0:T(1024)S(1)} %add.153, f32[5120]{0:T(1024)S(1)} %mul.71, bf16[256,5120]{1,0:T(8,128)(2,1)} %param.13, ...), kind=kOutput, calls=%fused_computation.1 | convolution fusion | flops 1103183872 | bytes 21602944 | tf_op jit(solution)/shard_map/dot_general | solution.py:286
  39.7 7.8 %convert_element_type.31 = bf16[256,8,4,256]{3,2,1,0:T(4,128)(2,1)} reshape(bf16[256,8192]{1,0:T(8,128)(2,1)} %convolution_convert_fusion) | data formatting | bytes 8388608 | tf_op jit(solution)/shard_map/convert_element_type | solution.py:312
  47.5 3.2 %copy.23 = bf16[256,4,8,256]{3,2,1,0:T(8,128)(2,1)S(1)} copy(bf16[256,4,8,256]{3,1,2,0:T(4,128)(2,1)} %bitcast.55) | data formatting | bytes 8388608 | tf_op jit(solution)/shard_map/convert_element_type | solution.py:312
  50.7 0.0 copy-start.9
  50.7 0.0 copy-start.7
  50.7 0.0 copy-start.8
  50.7 6.2 %copy.28 = bf16[32,8,32,256]{3,1,2,0:T(8,128)(2,1)} copy(bf16[32,8,32,256]{3,2,1,0:T(8,128)(2,1)S(1)} %bitcast.56) | data formatting | bytes 8388608
  57.0 0.0 copy-start.3
  57.0 0.0 copy-start.2
  57.0 0.0 reduce-scatter.2.cloned.1.call-update
  57.0 0.1 ge.66
  57.1 0.0 copy-done.9
  57.1 0.0 copy-done.7
  57.1 0.0 copy-done.8
  57.1 0.1 select_reduce_fusion
  57.2 0.4 fusion.45
  57.6 0.1 compare_select_fusion.3
  57.7 0.1 copy.24
  57.8 0.1 reshape.390
  57.8 0.1 fusion.48
  57.9 0.1 copy.22
  58.0 0.8 dynamic_slice.15
  58.8 0.3 fusion.49
  59.1 79.6 %reduce-scatter.2.cloned.1.call-done = bf16[256,256]{1,0:T(8,128)(2,1)} async-done(((bf16[256,8192]{1,0:T(8,128)(2,1)}), bf16[256,256]{1,0:T(8,128)(2,1)}) %reduce-scatter.2.cloned.1.call-update) | async-done | bytes 131088 | tf_op jit(solution)/shard_map/reduce_scatter | solution.py:311
  138.7 0.9 add_convert_fusion.4
  139.6 2.0 gather_fusion
  141.6 0.8 broadcast_select_fusion
  142.4 6.6 %all-to-all-start = ((bf16[16,32,256]{2,1,0:T(8,128)(2,1)}), bf16[16,32,256]{2,1,0:T(8,128)(2,1)S(1)}, u32[]{:S(2)}, u32[]{:S(2)}) async-start(bf16[16,32,256]{2,1,0:T(8,128)(2,1)} %broadcast_select_fusion), calls=%async_computation.1 | async-start | bytes 524288 | tf_op jit(solution)/shard_map/all_to_all | solution.py:319
  149.1 0.1 fusion.51
  149.1 0.1 and.25
  149.2 0.6 broadcast.395
  149.8 0.0 copy-done.3
  149.8 0.8 reduce.9
  150.6 0.6 reshape.385.gain_ref
  151.2 1.5 all-to-all-done
  152.7 0.2 copy.25
  153.0 0.0 copy-done.2
  153.0 0.8 bitcast_select_fusion.stream_ref
  153.8 0.0 copy-start.1
  153.8 115.6 %shard_map.127 = bf16[128,1024]{1,0:T(8,128)(2,1)} custom-call(bf16[128,1024]{1,0:T(8,128)(2,1)} %bitcast_select_fusion.stream_ref, f32[8,1024]{1,0:T(8,128)} %reshape.385.gain_ref, bf16[8,1024,1024]{2,1,0:T(8,128)(2,1)} %bitcast.53), custom_call_target="tpu_custom_call" | custom-call | tf_op jit(solution)/shard_map/pallas_call | solution.py:225
  269.4 1.7 copy.31
  271.1 0.0 copy-done.1
  (16 shorter events, 0.2 us)
Async XLA Ops:
  6.5 21.9 %copy-start = (bf16[160,8192]{1,0:T(8,128)(2,1)S(1)}, bf16[160,8192]{1,0:T(8,128)(2,1)}, u32[]{:S(2)}) copy-start(bf16[160,8192]{1,0:T(8,128)(2,1)} %param.18) | copy-start | bytes 7864324
  6.5 132.2 %reduce-scatter.2.cloned.1.call-start = ((), (), s32[]{:S(2)}) async-start(), calls=%async_computation.2 | async-start | bytes 4325376 | tf_op jit(solution)/shard_map/reduce_scatter | solution.py:311
  25.1 3.3 %copy-start.4 = (f32[1280]{0:T(1024)S(1)}, f32[1280]{0:T(1024)}, u32[]{:S(2)}) copy-start(f32[1280]{0:T(1024)} %param.15) | copy-start | bytes 15364
  25.1 3.3 %copy-start.5 = (f32[1280]{0:T(1024)S(1)}, f32[1280]{0:T(1024)}, u32[]{:S(2)}) copy-start(f32[1280]{0:T(1024)} %param.14) | copy-start | bytes 15364
  25.1 3.4 %copy-start.6 = (f32[160]{0:T(256)S(1)}, f32[160]{0:T(256)}, u32[]{:S(2)}) copy-start(f32[160]{0:T(256)} %param.17) | copy-start | bytes 1924
  50.7 6.4 %copy-start.9 = (s32[4,64]{1,0:T(4,128)S(1)}, s32[4,64]{1,0:T(4,128)}, u32[]{:S(2)}) copy-start(s32[4,64]{1,0:T(4,128)} %param.23) | copy-start | bytes 3076
  50.7 6.4 %copy-start.7 = (s32[4,64]{1,0:T(4,128)S(1)}, s32[4,64]{1,0:T(4,128)}, u32[]{:S(2)}) copy-start(s32[4,64]{1,0:T(4,128)} %param.24) | copy-start | bytes 3076
  50.7 6.4 %copy-start.8 = (s32[4,64]{1,0:T(4,128)S(1)}, s32[4,64]{1,0:T(4,128)}, u32[]{:S(2)}) copy-start(s32[4,64]{1,0:T(4,128)} %param.25) | copy-start | bytes 3076
  57.0 92.9 %copy-start.3 = (f32[1,8192]{1,0:T(1,128)S(1)}, f32[1,8192]{1,0:T(1,128)}, u32[]{:S(2)}) copy-start(f32[1,8192]{1,0:T(1,128)} %param.21) | copy-start | bytes 98308
  57.0 96.0 %copy-start.2 = (bf16[1,1,128,1024]{3,2,1,0:T(8,128)(2,1)S(1)}, bf16[1,1,128,1024]{3,2,1,0:T(8,128)(2,1)}, u32[]{:S(2)}) copy-start(bf16[1,1,128,1024]{3,2,1,0:T(8,128)(2,1)} %param.20) | copy-start | bytes 786436
  142.4 10.3 %all-to-all-start = ((bf16[16,32,256]{2,1,0:T(8,128)(2,1)}), bf16[16,32,256]{2,1,0:T(8,128)(2,1)S(1)}, u32[]{:S(2)}, u32[]{:S(2)}) async-start(bf16[16,32,256]{2,1,0:T(8,128)(2,1)} %broadcast_select_fusion), calls=%async_computation.1 | async-start | bytes 524288 | tf_op jit(solution)/shard_map/all_to_all | solution.py:319
  153.8 117.3 %copy-start.1 = (bf16[160,8192]{1,0:T(8,128)(2,1)S(1)}, bf16[160,8192]{1,0:T(8,128)(2,1)}, u32[]{:S(2)}) copy-start(bf16[160,8192]{1,0:T(8,128)(2,1)} %param.18) | copy-start | bytes 7864324
Sparse Core Ops, SparseCore 0:
  57.1 81.5 reduce-scatter.1

commit v2 on v1

v2 whole, which is shorter than its diff:
```python
import jax
import jax.numpy as jnp
from jax import lax
from jax.experimental import pallas as pl
from jax.experimental.pallas import tpu as pltpu
from jax.sharding import PartitionSpec as P

SLOT = 8
K_PAIR = 4
ROWS = 64
PARTS = 2
MESH = pl.DeviceIdType.MESH
F32 = jnp.float32
BF16 = jnp.bfloat16


def place(slots, sizes, places, starts_at):
    count = sizes.shape[1]
    images = lax.broadcasted_iota(jnp.int32, (slots.shape[0], count), 1)
    match = places == slots // SLOT

    def picked(values):
        return jnp.sum(jnp.where(match, values, 0), axis=1, keepdims=True)

    image = picked(images)
    extent = picked(sizes)
    first = jnp.sum(jnp.where(images < image, sizes, 0), axis=1, keepdims=True)
    column = lax.rem(slots, SLOT) - jnp.minimum(picked(starts_at), SLOT - extent)
    return first + column, (column >= 0) & (column < extent)


def kernel(
    patches_hbm, ln_gain_ref, ln_bias_ref, w_in_hbm, b_in_ref, w_out_hbm, b_out_ref, text_ref,
    gain_ref, weight_hbm, sizes_ref, places_ref, offsets_ref,
    out_ref,
    patches, encoded, w_in, w_out, hidden, out1, in1, out2, in2, own, piece, picks, placed, images, text, texts,
    shards, weight, total, squares, results,
    load_sem, w_out_sem, hid_sem, rs1_sent, rs1_got, rs2_sent, rs2_got, text_sent, text_got, place_sent, image_got,
    weight_sem, got, sent, home_sem,
):
    section, dp, mp = (lax.axis_index(a) for a in ("section", "dp", "mp"))
    n_section, n_dp, n_mp = (lax.axis_size(a) for a in ("section", "dp", "mp"))
    n_ring = n_mp // 2
    chip, core = mp // 2, lax.rem(mp, 2)
    chunks, _, rows, width = shards.shape
    per_micro = chunks // n_section
    seq_len = rows * per_micro
    per_group = K_PAIR * SLOT
    rows_enc, inner = patches.shape
    features = ln_gain_ref.shape[1]
    half_rows = rows_enc // 2
    sub = width // n_section
    span = width // PARTS

    def at(chip_pos, core_pos):
        return lax.rem(chip_pos + n_ring, n_ring) * 2 + core_pos

    ahead, behind = at(chip + 1, core), at(chip - 1, core)
    sibling = at(chip, 1 - core)
    turn = 1 - 2 * core
    onward, source = at(chip + turn, core), at(chip - turn, core)
    far = at(chip + 2, core)

    def load(src, dst, slot):
        return pltpu.make_async_copy(src, dst, load_sem.at[slot])

    def load_weight(idx):
        return pltpu.make_async_copy(weight_hbm.at[idx], weight.at[idx], weight_sem.at[idx])

    barrier = pltpu.get_barrier_semaphore()

    def greet(**target):
        pl.semaphore_signal(barrier, inc=1, device_id=target, device_id_type=MESH)

    load(w_in_hbm, w_in, 0).start()
    load(patches_hbm, patches, 1).start()
    for partner in (ahead, behind, sibling):
        greet(mp=partner)

    @pl.when(section == 0)
    def _():
        for there in range(n_section):
            for hop in range(n_dp):
                if there or hop:
                    greet(section=there, dp=lax.rem(dp + hop, n_dp))

    @pl.when(section != 0)
    def _():
        for hop in range(n_dp):
            greet(section=0, dp=lax.rem(dp + hop, n_dp))
        for hop in range(1, n_section):
            there = lax.rem(section + hop, n_section)

            @pl.when(there != 0)
            def _():
                greet(section=there)

    def w_out_block(chip_pos, core_pos):
        columns = pl.multiple_of((chip_pos * 2 + core_pos) * width, width)
        return w_out_hbm.at[:, pl.ds(columns, width)]

    def w_out_own(chip_pos):
        return pltpu.make_async_copy(w_out_block(chip_pos, core), w_out.at[0, chip_pos], w_out_sem.at[0, chip_pos])

    def w_out_other(chip_pos):
        return pltpu.make_async_remote_copy(
            src_ref=w_out_block(chip_pos, 1 - core), dst_ref=w_out.at[1, chip_pos],
            send_sem=w_out_sem.at[1, chip_pos], recv_sem=w_out_sem.at[2, chip_pos],
            device_id={"mp": sibling}, device_id_type=MESH,
        )

    for chip_pos in range(n_ring):
        w_out_own(chip_pos).start()

    position = lax.broadcasted_iota(jnp.int32, (seq_len, 1), 0)
    group = position // per_group
    owner = section * n_dp + dp
    slots = owner * per_group + lax.rem(position, per_group)

    def by_group(ref):
        values = jnp.broadcast_to(ref[0:1, :], (seq_len, ref.shape[1]))
        for e in range(1, n_dp):
            values = jnp.where(group == e, ref[e : e + 1, :], values)
        return values

    _, covered = place(slots, by_group(sizes_ref), by_group(places_ref), by_group(offsets_ref))
    text[...] = jnp.where(covered, jnp.zeros((), F32), text_ref[...].astype(F32)).astype(BF16)

    everywhere = lax.broadcasted_iota(jnp.int32, (n_section * n_dp * per_group, 1), 0)
    mine = pl.ds(dp, 1)
    row, covered = place(everywhere, sizes_ref[mine, :], places_ref[mine, :], offsets_ref[mine, :])
    candidates = lax.broadcasted_iota(jnp.int32, (everywhere.shape[0], rows_enc), 1)
    picks[...] = jnp.where((candidates == row) & covered, 1.0, 0.0).astype(BF16)

    pl.semaphore_wait(barrier, jnp.where(section == 0, n_section * n_dp + 2, n_dp + n_section + 1))

    for chip_pos in range(n_ring):
        w_out_other(chip_pos).start()

    def feed():
        return pltpu.make_async_remote_copy(
            src_ref=text, dst_ref=texts.at[section],
            send_sem=text_sent, recv_sem=text_got.at[section],
            device_id={"section": 0}, device_id_type=MESH,
        )

    @pl.when(section != 0)
    def _():
        feed().start()

    @pl.when(section == 0)
    def _():
        pltpu.make_async_copy(text, texts.at[0], text_got.at[0]).start()

    for idx in range(n_mp):
        load_weight(idx).start()

    load(patches_hbm, patches, 1).wait()
    block = 16

    def norm(b, carry):
        here = pl.ds(pl.multiple_of(b * block, block), block)
        for q in range(inner // features):
            columns = slice(q * features, (q + 1) * features)
            values = patches[here, columns].astype(F32)
            centre = values - jnp.mean(values, axis=-1, keepdims=True)
            spread = jnp.mean(centre * centre, axis=-1, keepdims=True)
            normed = centre * lax.rsqrt(spread + 1e-06) * ln_gain_ref[...] + ln_bias_ref[...]
            encoded[here, columns] = normed.astype(BF16)
        return carry

    lax.fori_loop(0, rows_enc // block, norm, 0)
    load(w_in_hbm, w_in, 0).wait()
    before = lax.dot_general(
        encoded[...], w_in[...], (((1,), (1,)), ((), ())), preferred_element_type=F32
    ) + b_in_ref[...]
    hidden[0] = (0.5 * before * (1.0 + lax.erf(before * (0.5**0.5)))).astype(BF16)

    swap = pltpu.make_async_remote_copy(
        src_ref=hidden.at[0], dst_ref=hidden.at[1], send_sem=hid_sem.at[0], recv_sem=hid_sem.at[1],
        device_id={"mp": sibling}, device_id_type=MESH,
    )
    swap.start()
    for chip_pos in range(n_ring):
        w_out_own(chip_pos).wait()
    for chip_pos in range(n_ring):
        w_out_other(chip_pos).wait_recv()
    swap.wait_recv()

    def along(axis, delta):
        if axis:
            return {"section": lax.rem(section + delta + n_section, n_section)}
        return {"mp": at(chip + delta, core)}

    def spot(axis, delta):
        return lax.rem((section if axis else chip) + delta + n_ring, n_ring)

    def partial(h, idx, p):
        def product(k, chip_pos, columns):
            return jnp.dot(
                hidden[k, h * half_rows : (h + 1) * half_rows, :], w_out[k, chip_pos, :, columns],
                preferred_element_type=F32,
            )

        if h == 0:
            columns = slice(p * span, (p + 1) * span)
            return product(0, idx, columns) + product(1, idx, columns)
        columns = pl.ds(pl.multiple_of(idx * sub, sub), sub)
        count = span // sub
        return jnp.concatenate(
            [product(0, z, columns) + product(1, z, columns) for z in range(p * count, (p + 1) * count)], axis=1
        )

    def rs1(h, kind, p, delta):
        return pltpu.make_async_remote_copy(
            src_ref=out1.at[h, kind, p], dst_ref=in1.at[h, kind, p],
            send_sem=rs1_sent.at[h, kind, p], recv_sem=rs1_got.at[h, kind, p],
            device_id=along(h, delta), device_id_type=MESH,
        )

    def rs2(h, kind, delta):
        return pltpu.make_async_remote_copy(
            src_ref=out2.at[h, kind], dst_ref=in2.at[h, kind],
            send_sem=rs2_sent.at[h, kind], recv_sem=rs2_got.at[h, kind],
            device_id=along(1 - h, delta), device_id_type=MESH,
        )

    FAR, NEAR, SUM = 0, 1, 2
    for p in range(PARTS):
        for h in range(2):
            out1[h, FAR, p] = partial(h, spot(h, 2), p).astype(BF16)
            rs1(h, FAR, p, turn).start()
    for p in range(PARTS):
        for h in range(2):
            out1[h, NEAR, p] = partial(h, spot(h, -turn), p).astype(BF16)
            rs1(h, NEAR, p, -turn).start()
    for p in range(PARTS):
        for h in range(2):
            value = partial(h, spot(h, turn), p)
            rs1(h, FAR, p, turn).wait_recv()
            out1[h, SUM, p] = (value + in1[h, FAR, p].astype(F32)).astype(BF16)
            rs1(h, SUM, p, turn).start()
    for p in range(PARTS):
        for h in range(2):
            own[h, :, p * span : (p + 1) * span] = partial(h, spot(h, 0), p)
    for p in range(PARTS):
        for h in range(2):
            columns = slice(p * span, (p + 1) * span)
            rs1(h, NEAR, p, -turn).wait_recv()
            rs1(h, SUM, p, turn).wait_recv()
            own[h, :, columns] += in1[h, NEAR, p].astype(F32) + in1[h, SUM, p].astype(F32)

    def own_block(h, delta):
        columns = pl.ds(pl.multiple_of(spot(1 - h, delta) * sub, sub), sub)
        return own[h, :, columns]

    for h in range(2):
        out2[h, FAR] = own_block(h, 2).astype(BF16)
        rs2(h, FAR, turn).start()
        out2[h, NEAR] = own_block(h, -turn).astype(BF16)
        rs2(h, NEAR, -turn).start()
    for h in range(2):
        value = own_block(h, turn)
        rs2(h, FAR, turn).wait_recv()
        out2[h, SUM] = (value + in2[h, FAR].astype(F32)).astype(BF16)
        rs2(h, SUM, turn).start()
    bias = b_out_ref[pl.ds(mp * n_section + section, 1), :]
    for h in range(2):
        value = own_block(h, 0)
        rs2(h, NEAR, -turn).wait_recv()
        rs2(h, SUM, turn).wait_recv()
        value = value + in2[h, NEAR].astype(F32) + in2[h, SUM].astype(F32) + bias
        piece[h * half_rows : (h + 1) * half_rows, :] = value.astype(BF16)

    placed[...] = jnp.dot(picks[...], piece[...], preferred_element_type=F32).astype(BF16)

    def block_of(micro, seq):
        begin = pl.multiple_of((micro * n_dp + seq) * per_group, per_group)
        return placed.at[pl.ds(begin, per_group)]

    def landing(micro):
        return images.at[
            micro, pl.ds(pl.multiple_of(dp * per_group, per_group), per_group),
            pl.ds(pl.multiple_of(section * sub, sub), sub),
        ]

    part_of = dp * per_group // rows

    def deliver(micro, hop):
        seq = lax.rem(dp + hop, n_dp)
        return pltpu.make_async_remote_copy(
            src_ref=block_of(micro, seq), dst_ref=landing(micro),
            send_sem=place_sent.at[micro, hop], recv_sem=image_got.at[micro * per_micro + part_of],
            device_id={"section": 0, "dp": seq}, device_id_type=MESH,
        )

    for micro in range(n_section):
        for hop in range(n_dp):
            if hop:
                deliver(micro, hop).start()
            else:
                @pl.when(section != 0)
                def _():
                    deliver(micro, 0).start()

                @pl.when(section == 0)
                def _():
                    pltpu.make_async_copy(
                        block_of(micro, dp), landing(micro), image_got.at[micro * per_micro + part_of]
                    ).start()

    def shard_copy(t, idx, slot, **target):
        return pltpu.make_async_remote_copy(
            src_ref=shards.at[t, idx], dst_ref=shards.at[t, idx],
            send_sem=sent.at[t, slot], recv_sem=got.at[t, idx],
            device_id=target, device_id_type=MESH,
        )

    def arrival(t, idx):
        shard_copy(t, idx, 0, mp=sibling).wait_recv()

    def enter(t):
        micro, part = t // per_micro, lax.rem(t, per_micro)
        here = pl.ds(pl.multiple_of(part * rows, rows), rows)

        @pl.when(part == 0)
        def _():
            pltpu.make_async_remote_copy(
                src_ref=text, dst_ref=texts.at[micro], send_sem=text_sent, recv_sem=text_got.at[micro],
                device_id={"section": 0}, device_id_type=MESH,
            ).wait_recv()

        pltpu.make_async_remote_copy(
            src_ref=images.at[micro, here], dst_ref=images.at[micro, here],
            send_sem=text_sent, recv_sem=image_got.at[t],
            device_id={"section": 0}, device_id_type=MESH,
        ).wait_recv()
        shards[t, mp] = (images[micro, here, :].astype(F32) + texts[micro, here, :].astype(F32)).astype(BF16)

    def pass_on(t):
        return pltpu.make_async_remote_copy(
            src_ref=results.at[t], dst_ref=shards.at[t, mp],
            send_sem=sent.at[t, 7], recv_sem=got.at[t, mp],
            device_id={"section": section + 1}, device_id_type=MESH,
        )

    def bring_home(t):
        half = lax.rem(t, per_micro)
        return pltpu.make_async_remote_copy(
            src_ref=results.at[t], dst_ref=out_ref.at[pl.ds(pl.multiple_of(half * rows, rows), rows)],
            send_sem=sent.at[t, 7], recv_sem=home_sem.at[half],
            device_id={"section": t // per_micro}, device_id_type=MESH,
        )

    def add(t, idx):
        values = shards[t, idx].astype(F32)
        square = values * values
        lanes = squares[...]
        for j in range(0, width, 128):
            lanes = lanes + square[:, j : j + 128]
        squares[...] = lanes
        scaled = (values * gain_ref[pl.ds(idx, 1), :]).astype(BF16)
        total[...] += jnp.dot(scaled, weight[idx], preferred_element_type=F32)

    last = n_section - 1

    def turn_body(i, carry):
        t = i - 1

        @pl.when(i < chunks)
        def _():
            @pl.when(section == 0)
            def _():
                enter(i)

            @pl.when(section != 0)
            def _():
                arrival(i, mp)

            shard_copy(i, mp, 0, mp=onward).start()
            shard_copy(i, mp, 1, mp=source).start()
            shard_copy(i, mp, 2, mp=sibling).start()

        @pl.when(i == 1)
        def _():
            for idx in range(n_mp):
                load_weight(idx).wait()

        @pl.when(i > 0)
        def _():
            total[...] = jnp.zeros_like(total)
            squares[...] = jnp.zeros_like(squares)
            add(t, mp)
            add(t, source)
            add(t, onward)
            arrival(t, far)
            shard_copy(t, far, 3, mp=sibling).start()
            add(t, far)
            for step in (0, 1, -1):
                idx = at(chip + step, 1 - core)
                arrival(t, idx)
                add(t, idx)

        @pl.when(i < chunks)
        def _():
            arrival(i, source)
            shard_copy(i, source, 4, mp=onward).start()
            shard_copy(i, source, 5, mp=sibling).start()
            arrival(i, onward)
            shard_copy(i, onward, 6, mp=sibling).start()

        @pl.when(i > 0)
        def _():
            idx = at(chip + 2, 1 - core)
            arrival(t, idx)
            add(t, idx)
            square = jnp.sum(squares[...], axis=-1, keepdims=True) * (1.0 / (n_mp * width))
            update = total[...] * lax.rsqrt(square + 1e-06)
            result = (shards[t, mp].astype(F32) + update).astype(BF16)
            results[t] = result

            @pl.when(section < last)
            def _():
                pass_on(t).start()

            @pl.when((section == last) & (t < last * per_micro))
            def _():
                bring_home(t).start()

            @pl.when((section == last) & (t >= last * per_micro))
            def _():
                half = lax.rem(t, per_micro)
                out_ref[pl.ds(pl.multiple_of(half * rows, rows), rows)] = result

        return carry

    lax.fori_loop(0, chunks + 1, turn_body, 0)

    @pl.when(section < last)
    def _():
        for half in range(per_micro):
            bring_home(half).wait_recv()

    for chip_pos in range(n_ring):
        w_out_other(chip_pos).wait_send()
    swap.wait_send()
    for h in range(2):
        for kind in range(3):
            for p in range(PARTS):
                rs1(h, kind, p, 1).wait_send()
            rs2(h, kind, 1).wait_send()
    for micro in range(n_section):
        for hop in range(1, n_dp):
            deliver(micro, hop).wait_send()

    @pl.when(section != 0)
    def _():
        feed().wait_send()
        for micro in range(n_section):
            deliver(micro, 0).wait_send()

    def settle(t, carry):
        for slot in range(7):
            shard_copy(t, mp, slot, mp=sibling).wait_send()

        @pl.when((section < last) | (t < last * per_micro))
        def _():
            shard_copy(t, mp, 7, mp=sibling).wait_send()

        return carry

    lax.fori_loop(0, chunks, settle, 0)


def per_device(
    n_section,
    n_dp,
    n_mp,
    patches,
    ln_gain,
    ln_bias,
    w_merge_in,
    b_merge_in,
    w_merge_out,
    b_merge_out,
    text_rows,
    section_gain,
    section_weight,
    image_sizes,
    placement,
    offsets,
):
    rows_enc, inner = patches.shape
    depth, features_out = w_merge_out.shape
    seq_len, width = text_rows.shape[2:]
    n_ring = n_mp // 2
    sub = width // n_section
    half = rows_enc // 2
    chunks = n_section * seq_len // ROWS
    per_micro = seq_len // ROWS
    slots = n_section * n_dp * K_PAIR * SLOT
    dma = pltpu.SemaphoreType.DMA
    vmem = pl.BlockSpec(memory_space=pltpu.VMEM)
    hbm = pl.BlockSpec(memory_space=pl.ANY)
    out = pl.pallas_call(
        kernel,
        out_shape=jax.ShapeDtypeStruct((seq_len, width), BF16),
        in_specs=[hbm, vmem, vmem, hbm, vmem, hbm, vmem, vmem, vmem, hbm, vmem, vmem, vmem],
        out_specs=vmem,
        scratch_shapes=[
            pltpu.VMEM((rows_enc, inner), BF16),
            pltpu.VMEM((rows_enc, inner), BF16),
            pltpu.VMEM((depth, inner), BF16),
            pltpu.VMEM((2, n_ring, depth, width), BF16),
            pltpu.VMEM((2, rows_enc, depth), BF16),
            pltpu.VMEM((2, 3, PARTS, half, width // PARTS), BF16),
            pltpu.VMEM((2, 3, PARTS, half, width // PARTS), BF16),
            pltpu.VMEM((2, 3, half, sub), BF16),
            pltpu.VMEM((2, 3, half, sub), BF16),
            pltpu.VMEM((2, half, width), F32),
            pltpu.VMEM((rows_enc, sub), BF16),
            pltpu.VMEM((slots, rows_enc), BF16),
            pltpu.VMEM((slots, sub), BF16),
            pltpu.VMEM((n_section, seq_len, width), BF16),
            pltpu.VMEM((seq_len, width), BF16),
            pltpu.VMEM((n_section, seq_len, width), BF16),
            pltpu.VMEM((chunks, n_mp, ROWS, width), BF16),
            pltpu.VMEM((n_mp, width, width), BF16),
            pltpu.VMEM((ROWS, width), F32),
            pltpu.VMEM((ROWS, 128), F32),
            pltpu.VMEM((chunks, ROWS, width), BF16),
            dma((2,)),
            dma((3, n_ring)),
            dma((2,)),
            dma((2, 3, PARTS)),
            dma((2, 3, PARTS)),
            dma((2, 3)),
            dma((2, 3)),
            dma,
            dma((n_section,)),
            dma((n_section, n_dp)),
            dma((chunks,)),
            dma((n_mp,)),
            dma((chunks, n_mp)),
            dma((chunks, 8)),
            dma((per_micro,)),
        ],
        compiler_params=pltpu.CompilerParams(
            collective_id=0, has_side_effects=True, vmem_limit_bytes=60 * 2**20
        ),
    )(
        patches,
        ln_gain.reshape(1, -1),
        ln_bias.reshape(1, -1),
        w_merge_in.T,
        b_merge_in.reshape(1, -1),
        w_merge_out,
        b_merge_out.reshape(n_mp * n_section, sub),
        text_rows.reshape(seq_len, width),
        section_gain.reshape(n_mp, width),
        section_weight.reshape(n_mp, width, width),
        image_sizes,
        placement,
        offsets,
    )
    return out.reshape(1, 1, seq_len, width)


def solution(mesh):
    in_specs = (
        P("dp", None),
        P(),
        P(),
        P(None, ("section", "mp")),
        P(("section", "mp")),
        P(("section", "mp"), None),
        P(),
        P("section", "dp", None, "mp"),
        P("section", None),
        P("section", None, "mp"),
        P(),
        P(),
        P(),
    )
    out_specs = P("section", "dp", None, "mp")
    sizes = (mesh.shape["section"], mesh.shape["dp"], mesh.shape["mp"])

    def run(*arrays):
        return per_device(*sizes, *arrays)

    return jax.shard_map(run, mesh=mesh, in_specs=in_specs, out_specs=out_specs, check_vma=False)
```

time: 281 us -> 161 us (0.57)
  waiting for transfers between devices: 81.1 us -> 0 us
  Pallas kernels: 116 us -> 152 us
  local copies, waits for them, and re-layouts: 38.1 us -> 6.77 us
  between operations: 13.6 us -> 0.01 us
  matrix products: 11.2 us -> 0 us
  other arithmetic: 11.6 us -> 1.48 us
  starting transfers between devices: 6.63 us -> 0 us
    reduce_scatter x1 -> x0, waiting for transfers between devices: 79.6 us -> none  [per_device(): lax.psum_scatter(ordered.astype(jnp.bfloat16), ('section', 'mp'), scatter...]
    pallas_call x1, Pallas kernels: 116 us -> 152 us  [per_device(): pl.pallas_call(kernel, out_shape=jax.ShapeDtypeStruct((seq_len, width), B...]
    unnamed x26 -> x2, local copies, waits for them, and re-layouts: 15.1 us -> 2.18 us
    dot_general x1 -> x0, matrix products: 11.2 us -> none  [per_device(): jnp.dot(hidden, w_merge_out, preferred_element_type=jnp.float32)]
    convert_element_type x2 -> x0, local copies, waits for them, and re-layouts: 11 us -> none  [per_device(): ordered.astype(jnp.bfloat16)]
    reduce_sum x5 -> x0, other arithmetic: 8.01 us -> none  [the longest x1 4.02 us: layer_norm(): spread = jnp.mean(centre * centre, axis=-1, keepdims=True)]
    all_to_all x1 -> x0, starting transfers between devices: 6.62 us -> none  [per_device(): lax.all_to_all(outgoing, ('section', 'dp'), split_axis=0, concat_axis=0,...]
    reshape x2 -> x4, local copies, waits for them, and re-layouts: 7.09 us -> 4.58 us  [the longest x1 1.38 us: per_device(): b_merge_out.reshape(n_mp * n_section, sub)]
  transfers between devices with their start and end apart: 2 -> 0, of which waited for: 2 -> 0; matrix products, arithmetic and copies ran while one was open for 2% -> 0% of each run, Pallas kernels for 0% -> 0%
where the time goes in v2:
time: 161 us
  Pallas kernels  152 us (94%)
  local copies, waits for them, and re-layouts  6.77 us (4%)
    pallas_call x1, Pallas kernels, per_device(): pl.pallas_call(kernel, out_shape=jax.ShapeDtypeStruct((seq_len, width), B...  152 us

profile of v2, /device:TPU:31, one launch (start us, length us, event | category | flops | bytes accessed | tf_op | source)
XLA Modules:
  0.0 160.5 jit_solution(11556929206423457677)
XLA Ops:
  0.0 1.3 reshape.24.ln_gain_ref
  1.3 1.3 reshape.25.ln_bias_ref
  2.6 0.5 broadcast.3
  3.1 1.5 reduce.3
  4.6 0.6 reshape.29.gain_ref
  5.2 1.4 reshape.27.b_out_ref
  6.6 152.3 %shard_map.127 = bf16[128,1024]{1,0:T(8,128)(2,1)} custom-call(bf16[256,5120]{1,0:T(8,128)(2,1)} %patches_hbm.1, f32[1,1280]{1,0:T(1,128)} %reshape.24.ln_gain_ref, f32[1,1280]{1,0:T(1,128)} %reshape.25.ln_bias_ref, bf16[160,5120]{1,0:T(8,128)(2,1)} %bitcast.6, f32[1,160]{1,0:T(1,128)} %bitcast.9, bf16[160,8192]{1,0:T(8,128)(2,1)} %w_out_hbm.1, ...), custom_call_target="tpu_custom_call" | custom-call | tf_op jit(solution)/shard_map/pallas_call | solution.py:505
  158.9 1.7 %copy.15 = bf16[1,1,128,1024]{3,2,1,0:T(8,128)(2,1)} copy(bf16[1,1,128,1024]{3,2,1,0:T(8,128)(2,1)} %bitcast.7) | data formatting | bytes 524288

commit v3 on v2

--- a/solution.py
+++ b/solution.py
@@ -7,7 +7,9 @@
 
 SLOT = 8
 K_PAIR = 4
-ROWS = 64
+ROWS = 32
+TALL = 128
+LAG = 2
 PARTS = 2
 MESH = pl.DeviceIdType.MESH
 F32 = jnp.float32
@@ -33,8 +35,8 @@
     patches_hbm, ln_gain_ref, ln_bias_ref, w_in_hbm, b_in_ref, w_out_hbm, b_out_ref, text_ref,
     gain_ref, weight_hbm, sizes_ref, places_ref, offsets_ref,
     out_ref,
-    patches, encoded, w_in, w_out, hidden, out1, in1, out2, in2, own, piece, picks, placed, images, text, texts,
-    shards, weight, total, squares, results,
+    patches, encoded, w_in, w_out, w_lent, hidden, out1, in1, out2, in2, own, piece, picks, placed, images, text, texts,
+    shards, weight, tall, total, squares, results,
     load_sem, w_out_sem, hid_sem, rs1_sent, rs1_got, rs2_sent, rs2_got, text_sent, text_got, place_sent, image_got,
     weight_sem, got, sent, home_sem,
 ):
@@ -47,7 +49,7 @@
     seq_len = rows * per_micro
     per_group = K_PAIR * SLOT
     rows_enc, inner = patches.shape
-    features = ln_gain_ref.shape[1]
+    features = ln_gain_ref.shape[0] * 128
     half_rows = rows_enc // 2
     sub = width // n_section
     span = width // PARTS
@@ -102,13 +104,18 @@
     def w_out_own(chip_pos):
         return pltpu.make_async_copy(w_out_block(chip_pos, core), w_out.at[0, chip_pos], w_out_sem.at[0, chip_pos])
 
+    def w_out_fetch(chip_pos):
+        return pltpu.make_async_copy(w_out_block(chip_pos, 1 - core), w_lent.at[chip_pos], w_out_sem.at[3, chip_pos])
+
     def w_out_other(chip_pos):
         return pltpu.make_async_remote_copy(
-            src_ref=w_out_block(chip_pos, 1 - core), dst_ref=w_out.at[1, chip_pos],
+            src_ref=w_lent.at[chip_pos], dst_ref=w_out.at[1, chip_pos],
             send_sem=w_out_sem.at[1, chip_pos], recv_sem=w_out_sem.at[2, chip_pos],
             device_id={"mp": sibling}, device_id_type=MESH,
         )
 
+    for chip_pos in range(n_ring):
+        w_out_fetch(chip_pos).start()
     for chip_pos in range(n_ring):
         w_out_own(chip_pos).start()
 
@@ -132,29 +139,14 @@
     candidates = lax.broadcasted_iota(jnp.int32, (everywhere.shape[0], rows_enc), 1)
     picks[...] = jnp.where((candidates == row) & covered, 1.0, 0.0).astype(BF16)
 
-    pl.semaphore_wait(barrier, jnp.where(section == 0, n_section * n_dp + 2, n_dp + n_section + 1))
-
-    for chip_pos in range(n_ring):
-        w_out_other(chip_pos).start()
-
-    def feed():
-        return pltpu.make_async_remote_copy(
-            src_ref=text, dst_ref=texts.at[section],
-            send_sem=text_sent, recv_sem=text_got.at[section],
-            device_id={"section": 0}, device_id_type=MESH,
-        )
-
-    @pl.when(section != 0)
-    def _():
-        feed().start()
-
-    @pl.when(section == 0)
-    def _():
-        pltpu.make_async_copy(text, texts.at[0], text_got.at[0]).start()
-
     for idx in range(n_mp):
         load_weight(idx).start()
 
+    def one_row(ref, begin, count):
+        return jnp.concatenate([ref[pl.ds(begin + k, 1), :] for k in range(count)], axis=1)
+
+    ln_gain = one_row(ln_gain_ref, 0, features // 128)
+    ln_bias = one_row(ln_bias_ref, 0, features // 128)
     load(patches_hbm, patches, 1).wait()
     block = 16
 
@@ -165,11 +157,17 @@
             values = patches[here, columns].astype(F32)
             centre = values - jnp.mean(values, axis=-1, keepdims=True)
             spread = jnp.mean(centre * centre, axis=-1, keepdims=True)
-            normed = centre * lax.rsqrt(spread + 1e-06) * ln_gain_ref[...] + ln_bias_ref[...]
+            normed = centre * lax.rsqrt(spread + 1e-06) * ln_gain + ln_bias
             encoded[here, columns] = normed.astype(BF16)
         return carry
 
     lax.fori_loop(0, rows_enc // block, norm, 0)
+    pl.semaphore_wait(barrier, jnp.where(section == 0, n_section * n_dp + 2, n_dp + n_section + 1))
+
+    for chip_pos in range(n_ring):
+        w_out_fetch(chip_pos).wait()
+        w_out_other(chip_pos).start()
+
     load(w_in_hbm, w_in, 0).wait()
     before = lax.dot_general(
         encoded[...], w_in[...], (((1,), (1,)), ((), ())), preferred_element_type=F32
@@ -264,7 +262,7 @@
         rs2(h, FAR, turn).wait_recv()
         out2[h, SUM] = (value + in2[h, FAR].astype(F32)).astype(BF16)
         rs2(h, SUM, turn).start()
-    bias = b_out_ref[pl.ds(mp * n_section + section, 1), :]
+    bias = one_row(b_out_ref, (mp * n_section + section) * (sub // 128), sub // 128)
     for h in range(2):
         value = own_block(h, 0)
         rs2(h, NEAR, -turn).wait_recv()
@@ -294,20 +292,46 @@
             device_id={"section": 0, "dp": seq}, device_id_type=MESH,
         )
 
-    for micro in range(n_section):
+    def feed():
+        return pltpu.make_async_remote_copy(
+            src_ref=text, dst_ref=texts.at[section],
+            send_sem=text_sent, recv_sem=text_got.at[section],
+            device_id={"section": 0}, device_id_type=MESH,
+        )
+
+    def keep(micro):
+        pltpu.make_async_copy(
+            block_of(micro, dp), landing(micro), image_got.at[micro * per_micro + part_of]
+        ).start()
+
+    def deliver_all(micro):
         for hop in range(n_dp):
-            if hop:
-                deliver(micro, hop).start()
-            else:
-                @pl.when(section != 0)
+            deliver(micro, hop).start()
+
+    def delivered(micro):
+        for hop in range(n_dp):
+            deliver(micro, hop).wait_send()
+
+    paced = 2
+
+    @pl.when(section == 0)
+    def _():
+        pltpu.make_async_copy(text, texts.at[0], text_got.at[0]).start()
+        keep(0)
+        for hop in range(1, n_dp):
+            deliver(0, hop).start()
+
+    @pl.when(section != 0)
+    def _():
+        for micro in range(n_section):
+            if micro:
+                @pl.when(section == micro)
                 def _():
-                    deliver(micro, 0).start()
-
-                @pl.when(section == 0)
-                def _():
-                    pltpu.make_async_copy(
-                        block_of(micro, dp), landing(micro), image_got.at[micro * per_micro + part_of]
-                    ).start()
+                    feed().start()
+
+            deliver_all(micro)
+            if micro < paced:
+                delivered(micro)
 
     def shard_copy(t, idx, slot, **target):
         return pltpu.make_async_remote_copy(
@@ -352,89 +376,94 @@
             device_id={"section": t // per_micro}, device_id_type=MESH,
         )
 
-    def add(t, idx):
+    def add(t, idx, first=False):
         values = shards[t, idx].astype(F32)
         square = values * values
-        lanes = squares[...]
-        for j in range(0, width, 128):
+        lanes = square[:, :128] if first else squares[...] + square[:, :128]
+        for j in range(128, width, 128):
             lanes = lanes + square[:, j : j + 128]
         squares[...] = lanes
-        scaled = (values * gain_ref[pl.ds(idx, 1), :]).astype(BF16)
-        total[...] += jnp.dot(scaled, weight[idx], preferred_element_type=F32)
+        gain = gain_ref[:, pl.ds(pl.multiple_of(idx * width, width), width)]
+        tall[idx, 0:rows] = (values * gain).astype(BF16)
+        update = jnp.dot(tall[idx], weight[idx], preferred_element_type=F32)[0:rows]
+        total[...] = update if first else total[...] + update
 
     last = n_section - 1
+    tall[...] = jnp.zeros_like(tall)
+
+    def begin(t):
+        @pl.when(section == 0)
+        def _():
+            enter(t)
+
+        @pl.when(section != 0)
+        def _():
+            arrival(t, mp)
+
+        shard_copy(t, mp, 0, mp=onward).start()
+        shard_copy(t, mp, 1, mp=source).start()
+        shard_copy(t, mp, 3, mp=far).start()
+        shard_copy(t, mp, 2, mp=sibling).start()
+
+    def share(t):
+        for slot, idx in ((4, source), (5, onward), (6, far)):
+            arrival(t, idx)
+            shard_copy(t, idx, slot, mp=sibling).start()
+
+    def multiply(t):
+        add(t, mp, True)
+        add(t, source)
+        add(t, onward)
+        add(t, far)
+        for step in (0, -1, 1, 2):
+            idx = at(chip + step * turn, 1 - core)
+            arrival(t, idx)
+            add(t, idx)
+        square = jnp.sum(squares[...], axis=-1, keepdims=True) * (1.0 / (n_mp * width))
+        update = total[...] * lax.rsqrt(square + 1e-06)
+        result = (shards[t, mp].astype(F32) + update).astype(BF16)
+        results[t] = result
+
+        @pl.when(section < last)
+        def _():
+            pass_on(t).start()
+
+        @pl.when((section == last) & (t < last * per_micro))
+        def _():
+            bring_home(t).start()
+
+        @pl.when((section == last) & (t >= last * per_micro))
+        def _():
+            part = lax.rem(t, per_micro)
+            out_ref[pl.ds(pl.multiple_of(part * rows, rows), rows)] = result
 
     def turn_body(i, carry):
-        t = i - 1
-
         @pl.when(i < chunks)
         def _():
-            @pl.when(section == 0)
-            def _():
-                enter(i)
-
-            @pl.when(section != 0)
-            def _():
-                arrival(i, mp)
-
-            shard_copy(i, mp, 0, mp=onward).start()
-            shard_copy(i, mp, 1, mp=source).start()
-            shard_copy(i, mp, 2, mp=sibling).start()
-
-        @pl.when(i == 1)
+            begin(i)
+
+        @pl.when((i == 1) & (section == 0))
+        def _():
+            for micro in range(1, n_section):
+                keep(micro)
+                for hop in range(1, n_dp):
+                    deliver(micro, hop).start()
+
+        @pl.when(i == LAG)
         def _():
             for idx in range(n_mp):
                 load_weight(idx).wait()
 
-        @pl.when(i > 0)
-        def _():
-            total[...] = jnp.zeros_like(total)
-            squares[...] = jnp.zeros_like(squares)
-            add(t, mp)
-            add(t, source)
-            add(t, onward)
-            arrival(t, far)
-            shard_copy(t, far, 3, mp=sibling).start()
-            add(t, far)
-            for step in (0, 1, -1):
-                idx = at(chip + step, 1 - core)
-                arrival(t, idx)
-                add(t, idx)
-
-        @pl.when(i < chunks)
-        def _():
-            arrival(i, source)
-            shard_copy(i, source, 4, mp=onward).start()
-            shard_copy(i, source, 5, mp=sibling).start()
-            arrival(i, onward)
-            shard_copy(i, onward, 6, mp=sibling).start()
-
-        @pl.when(i > 0)
-        def _():
-            idx = at(chip + 2, 1 - core)
-            arrival(t, idx)
-            add(t, idx)
-            square = jnp.sum(squares[...], axis=-1, keepdims=True) * (1.0 / (n_mp * width))
-            update = total[...] * lax.rsqrt(square + 1e-06)
-            result = (shards[t, mp].astype(F32) + update).astype(BF16)
-            results[t] = result
-
-            @pl.when(section < last)
-            def _():
-                pass_on(t).start()
-
-            @pl.when((section == last) & (t < last * per_micro))
-            def _():
-                bring_home(t).start()
-
-            @pl.when((section == last) & (t >= last * per_micro))
-            def _():
-                half = lax.rem(t, per_micro)
-                out_ref[pl.ds(pl.multiple_of(half * rows, rows), rows)] = result
+        t = i - LAG
+
+        @pl.when(t >= 0)
+        def _():
+            share(t)
+            multiply(t)
 
         return carry
 
-    lax.fori_loop(0, chunks + 1, turn_body, 0)
+    lax.fori_loop(0, chunks + LAG, turn_body, 0)
 
     @pl.when(section < last)
     def _():
@@ -449,15 +478,18 @@
             for p in range(PARTS):
                 rs1(h, kind, p, 1).wait_send()
             rs2(h, kind, 1).wait_send()
-    for micro in range(n_section):
-        for hop in range(1, n_dp):
-            deliver(micro, hop).wait_send()
+
+    @pl.when(section == 0)
+    def _():
+        for micro in range(n_section):
+            for hop in range(1, n_dp):
+                deliver(micro, hop).wait_send()
 
     @pl.when(section != 0)
     def _():
         feed().wait_send()
-        for micro in range(n_section):
-            deliver(micro, 0).wait_send()
+        for micro in range(paced, n_section):
+            delivered(micro)
 
     def settle(t, carry):
         for slot in range(7):
@@ -512,6 +544,7 @@
             pltpu.VMEM((rows_enc, inner), BF16),
             pltpu.VMEM((depth, inner), BF16),
             pltpu.VMEM((2, n_ring, depth, width), BF16),
+            pltpu.VMEM((n_ring, depth, width), BF16),
             pltpu.VMEM((2, rows_enc, depth), BF16),
             pltpu.VMEM((2, 3, PARTS, half, width // PARTS), BF16),
             pltpu.VMEM((2, 3, PARTS, half, width // PARTS), BF16),
@@ -526,11 +559,12 @@
             pltpu.VMEM((n_section, seq_len, width), BF16),
             pltpu.VMEM((chunks, n_mp, ROWS, width), BF16),
             pltpu.VMEM((n_mp, width, width), BF16),
+            pltpu.VMEM((n_mp, TALL, width), BF16),
             pltpu.VMEM((ROWS, width), F32),
             pltpu.VMEM((ROWS, 128), F32),
             pltpu.VMEM((chunks, ROWS, width), BF16),
             dma((2,)),
-            dma((3, n_ring)),
+            dma((4, n_ring)),
             dma((2,)),
             dma((2, 3, PARTS)),
             dma((2, 3, PARTS)),
@@ -550,14 +584,14 @@
         ),
     )(
         patches,
-        ln_gain.reshape(1, -1),
-        ln_bias.reshape(1, -1),
+        ln_gain.reshape(-1, 128),
+        ln_bias.reshape(-1, 128),
         w_merge_in.T,
         b_merge_in.reshape(1, -1),
         w_merge_out,
-        b_merge_out.reshape(n_mp * n_section, sub),
+        b_merge_out.reshape(-1, 128),
         text_rows.reshape(seq_len, width),
-        section_gain.reshape(n_mp, width),
+        section_gain,
         section_weight.reshape(n_mp, width, width),
         image_sizes,
         placement,

time: 161 us -> 145 us (0.901)
  Pallas kernels: 152 us -> 143 us
  local copies, waits for them, and re-layouts: 6.77 us -> 1.67 us
    pallas_call x1, Pallas kernels: 152 us -> 143 us  [per_device(): pl.pallas_call(kernel, out_shape=jax.ShapeDtypeStruct((seq_len, width), B...]
    reshape x4 -> x0, local copies, waits for them, and re-layouts: 4.58 us -> none  [the longest x1 1.38 us: per_device(): b_merge_out.reshape(n_mp * n_section, sub)]
where the time goes in v3:
time: 145 us
  Pallas kernels  143 us (99%)
  local copies, waits for them, and re-layouts  1.67 us (1%)
    pallas_call x1, Pallas kernels, per_device(): pl.pallas_call(kernel, out_shape=jax.ShapeDtypeStruct((seq_len, width), B...  143 us

profile of v3, /device:TPU:31, one launch (start us, length us, event | category | flops | bytes accessed | tf_op | source)
XLA Modules:
  0.0 145.0 jit_solution(12276896018785195117)
XLA Ops:
  0.0 143.4 %shard_map.127 = bf16[128,1024]{1,0:T(8,128)(2,1)} custom-call(bf16[256,5120]{1,0:T(8,128)(2,1)} %patches_hbm.1, f32[10,128]{1,0:T(8,128)} %bitcast.13, f32[10,128]{1,0:T(8,128)} %bitcast.14, bf16[160,5120]{1,0:T(8,128)(2,1)} %bitcast.9, f32[1,160]{1,0:T(1,128)} %bitcast.15, bf16[160,8192]{1,0:T(8,128)(2,1)} %w_out_hbm.1, f32[64,128]{1,0:T(8,128)} %bitcast.12, ...), custom_call_target="tpu_custom_call" | custom-call | tf_op jit(solution)/shard_map/pallas_call | solution.py:537
  143.4 1.7 %copy.15 = bf16[1,1,128,1024]{3,2,1,0:T(8,128)(2,1)} copy(bf16[1,1,128,1024]{3,2,1,0:T(8,128)(2,1)} %bitcast.10) | data formatting | bytes 524288

commit v4 on v3

--- a/solution.py
+++ b/solution.py
@@ -44,7 +44,7 @@
     n_section, n_dp, n_mp = (lax.axis_size(a) for a in ("section", "dp", "mp"))
     n_ring = n_mp // 2
     chip, core = mp // 2, lax.rem(mp, 2)
-    chunks, _, rows, width = shards.shape
+    chunks, _, _, rows, width = shards.shape
     per_micro = chunks // n_section
     seq_len = rows * per_micro
     per_group = K_PAIR * SLOT
@@ -60,8 +60,6 @@
     ahead, behind = at(chip + 1, core), at(chip - 1, core)
     sibling = at(chip, 1 - core)
     turn = 1 - 2 * core
-    onward, source = at(chip + turn, core), at(chip - turn, core)
-    far = at(chip + 2, core)
 
     def load(src, dst, slot):
         return pltpu.make_async_copy(src, dst, load_sem.at[slot])
@@ -216,11 +214,11 @@
             device_id=along(h, delta), device_id_type=MESH,
         )
 
-    def rs2(h, kind, delta):
+    def rs2(h, kind):
         return pltpu.make_async_remote_copy(
             src_ref=out2.at[h, kind], dst_ref=in2.at[h, kind],
             send_sem=rs2_sent.at[h, kind], recv_sem=rs2_got.at[h, kind],
-            device_id=along(1 - h, delta), device_id_type=MESH,
+            device_id=along(1 - h, kind + 1), device_id_type=MESH,
         )
 
     FAR, NEAR, SUM = 0, 1, 2
@@ -231,6 +229,7 @@
     for p in range(PARTS):
         for h in range(2):
             out1[h, NEAR, p] = partial(h, spot(h, -turn), p).astype(BF16)
+            rs1(h, FAR, p, turn).wait_send()
             rs1(h, NEAR, p, -turn).start()
     for p in range(PARTS):
         for h in range(2):
@@ -252,22 +251,16 @@
         columns = pl.ds(pl.multiple_of(spot(1 - h, delta) * sub, sub), sub)
         return own[h, :, columns]
 
-    for h in range(2):
-        out2[h, FAR] = own_block(h, 2).astype(BF16)
-        rs2(h, FAR, turn).start()
-        out2[h, NEAR] = own_block(h, -turn).astype(BF16)
-        rs2(h, NEAR, -turn).start()
-    for h in range(2):
-        value = own_block(h, turn)
-        rs2(h, FAR, turn).wait_recv()
-        out2[h, SUM] = (value + in2[h, FAR].astype(F32)).astype(BF16)
-        rs2(h, SUM, turn).start()
+    for kind in (1, 0, 2):
+        for h in range(2):
+            out2[h, kind] = own_block(h, kind + 1).astype(BF16)
+            rs2(h, kind).start()
     bias = one_row(b_out_ref, (mp * n_section + section) * (sub // 128), sub // 128)
     for h in range(2):
-        value = own_block(h, 0)
-        rs2(h, NEAR, -turn).wait_recv()
-        rs2(h, SUM, turn).wait_recv()
-        value = value + in2[h, NEAR].astype(F32) + in2[h, SUM].astype(F32) + bias
+        value = own_block(h, 0) + bias
+        for kind in (0, 2, 1):
+            rs2(h, kind).wait_recv()
+            value = value + in2[h, kind].astype(F32)
         piece[h * half_rows : (h + 1) * half_rows, :] = value.astype(BF16)
 
     placed[...] = jnp.dot(picks[...], piece[...], preferred_element_type=F32).astype(BF16)
@@ -333,15 +326,29 @@
             if micro < paced:
                 delivered(micro)
 
-    def shard_copy(t, idx, slot, **target):
-        return pltpu.make_async_remote_copy(
-            src_ref=shards.at[t, idx], dst_ref=shards.at[t, idx],
-            send_sem=sent.at[t, slot], recv_sem=got.at[t, idx],
-            device_id=target, device_id_type=MESH,
-        )
-
-    def arrival(t, idx):
-        shard_copy(t, idx, 0, mp=sibling).wait_recv()
+    def ring(step):
+        return lax.rem(chip + step * turn + n_ring, n_ring)
+
+    def shard_copy(t, step, slot):
+        return pltpu.make_async_remote_copy(
+            src_ref=shards.at[t, core, chip], dst_ref=shards.at[t, core, chip],
+            send_sem=sent.at[t, slot], recv_sem=got.at[t, slot],
+            device_id={"mp": at(chip + step * turn, core)}, device_id_type=MESH,
+        )
+
+    def entry(t):
+        return pltpu.make_async_remote_copy(
+            src_ref=results.at[t], dst_ref=shards.at[t, core, chip],
+            send_sem=sent.at[t, 4], recv_sem=got.at[t, 4],
+            device_id={"section": lax.rem(section + 1, n_section)}, device_id_type=MESH,
+        )
+
+    def lend(t):
+        return pltpu.make_async_remote_copy(
+            src_ref=shards.at[t, core], dst_ref=shards.at[t, core],
+            send_sem=sent.at[t, 3], recv_sem=got.at[t, 3],
+            device_id={"mp": sibling}, device_id_type=MESH,
+        )
 
     def enter(t):
         micro, part = t // per_micro, lax.rem(t, per_micro)
@@ -359,25 +366,19 @@
             send_sem=text_sent, recv_sem=image_got.at[t],
             device_id={"section": 0}, device_id_type=MESH,
         ).wait_recv()
-        shards[t, mp] = (images[micro, here, :].astype(F32) + texts[micro, here, :].astype(F32)).astype(BF16)
-
-    def pass_on(t):
-        return pltpu.make_async_remote_copy(
-            src_ref=results.at[t], dst_ref=shards.at[t, mp],
-            send_sem=sent.at[t, 7], recv_sem=got.at[t, mp],
-            device_id={"section": section + 1}, device_id_type=MESH,
-        )
+        shards[t, core, chip] = (images[micro, here, :].astype(F32) + texts[micro, here, :].astype(F32)).astype(BF16)
 
     def bring_home(t):
         half = lax.rem(t, per_micro)
         return pltpu.make_async_remote_copy(
             src_ref=results.at[t], dst_ref=out_ref.at[pl.ds(pl.multiple_of(half * rows, rows), rows)],
-            send_sem=sent.at[t, 7], recv_sem=home_sem.at[half],
+            send_sem=sent.at[t, 4], recv_sem=home_sem.at[half],
             device_id={"section": t // per_micro}, device_id_type=MESH,
         )
 
-    def add(t, idx, first=False):
-        values = shards[t, idx].astype(F32)
+    def add(t, core_pos, chip_pos, first=False):
+        idx = chip_pos * 2 + core_pos
+        values = shards[t, core_pos, chip_pos].astype(F32)
         square = values * values
         lanes = square[:, :128] if first else squares[...] + square[:, :128]
         for j in range(128, width, 128):
@@ -398,35 +399,31 @@
 
         @pl.when(section != 0)
         def _():
-            arrival(t, mp)
-
-        shard_copy(t, mp, 0, mp=onward).start()
-        shard_copy(t, mp, 1, mp=source).start()
-        shard_copy(t, mp, 3, mp=far).start()
-        shard_copy(t, mp, 2, mp=sibling).start()
+            entry(t).wait_recv()
+
+        shard_copy(t, 1, 0).start()
+        shard_copy(t, -1, 1).start()
+        shard_copy(t, 2, 2).start()
 
     def share(t):
-        for slot, idx in ((4, source), (5, onward), (6, far)):
-            arrival(t, idx)
-            shard_copy(t, idx, slot, mp=sibling).start()
+        for slot in range(3):
+            shard_copy(t, 1, slot).wait_recv()
+        lend(t).start()
 
     def multiply(t):
-        add(t, mp, True)
-        add(t, source)
-        add(t, onward)
-        add(t, far)
-        for step in (0, -1, 1, 2):
-            idx = at(chip + step * turn, 1 - core)
-            arrival(t, idx)
-            add(t, idx)
+        for step in range(n_ring):
+            add(t, core, ring(step), step == 0)
+        lend(t).wait_recv()
+        for step in range(n_ring):
+            add(t, 1 - core, ring(step))
         square = jnp.sum(squares[...], axis=-1, keepdims=True) * (1.0 / (n_mp * width))
         update = total[...] * lax.rsqrt(square + 1e-06)
-        result = (shards[t, mp].astype(F32) + update).astype(BF16)
+        result = (shards[t, core, chip].astype(F32) + update).astype(BF16)
         results[t] = result
 
         @pl.when(section < last)
         def _():
-            pass_on(t).start()
+            entry(t).start()
 
         @pl.when((section == last) & (t < last * per_micro))
         def _():
@@ -475,9 +472,10 @@
     swap.wait_send()
     for h in range(2):
         for kind in range(3):
-            for p in range(PARTS):
-                rs1(h, kind, p, 1).wait_send()
-            rs2(h, kind, 1).wait_send()
+            if kind != FAR:
+                for p in range(PARTS):
+                    rs1(h, kind, p, 1).wait_send()
+            rs2(h, kind).wait_send()
 
     @pl.when(section == 0)
     def _():
@@ -492,12 +490,13 @@
             delivered(micro)
 
     def settle(t, carry):
-        for slot in range(7):
-            shard_copy(t, mp, slot, mp=sibling).wait_send()
+        for slot in range(3):
+            shard_copy(t, 1, slot).wait_send()
+        lend(t).wait_send()
 
         @pl.when((section < last) | (t < last * per_micro))
         def _():
-            shard_copy(t, mp, 7, mp=sibling).wait_send()
+            entry(t).wait_send()
 
         return carry
 
@@ -557,7 +556,7 @@
             pltpu.VMEM((n_section, seq_len, width), BF16),
             pltpu.VMEM((seq_len, width), BF16),
             pltpu.VMEM((n_section, seq_len, width), BF16),
-            pltpu.VMEM((chunks, n_mp, ROWS, width), BF16),
+            pltpu.VMEM((chunks, 2, n_ring, ROWS, width), BF16),
             pltpu.VMEM((n_mp, width, width), BF16),
             pltpu.VMEM((n_mp, TALL, width), BF16),
             pltpu.VMEM((ROWS, width), F32),
@@ -575,8 +574,8 @@
             dma((n_section, n_dp)),
             dma((chunks,)),
             dma((n_mp,)),
-            dma((chunks, n_mp)),
-            dma((chunks, 8)),
+            dma((chunks, 5)),
+            dma((chunks, 5)),
             dma((per_micro,)),
         ],
         compiler_params=pltpu.CompilerParams(

time: 145 us -> 134 us (0.924)
  Pallas kernels: 143 us -> 132 us
    pallas_call x1, Pallas kernels: 143 us -> 132 us  [per_device(): pl.pallas_call(kernel, out_shape=jax.ShapeDtypeStruct((seq_len, width), B...]
where the time goes in v4:
time: 134 us
  Pallas kernels  132 us (99%)
  local copies, waits for them, and re-layouts  1.67 us (1%)
    pallas_call x1, Pallas kernels, per_device(): pl.pallas_call(kernel, out_shape=jax.ShapeDtypeStruct((seq_len, width), B...  132 us

profile of v4, /device:TPU:31, one launch (start us, length us, event | category | flops | bytes accessed | tf_op | source)
XLA Modules:
  0.0 133.8 jit_solution(5202923738618047838)
XLA Ops:
  0.0 132.1 %shard_map.127 = bf16[128,1024]{1,0:T(8,128)(2,1)} custom-call(bf16[256,5120]{1,0:T(8,128)(2,1)} %patches_hbm.1, f32[10,128]{1,0:T(8,128)} %bitcast.13, f32[10,128]{1,0:T(8,128)} %bitcast.14, bf16[160,5120]{1,0:T(8,128)(2,1)} %bitcast.9, f32[1,160]{1,0:T(1,128)} %bitcast.15, bf16[160,8192]{1,0:T(8,128)(2,1)} %w_out_hbm.1, f32[64,128]{1,0:T(8,128)} %bitcast.12, ...), custom_call_target="tpu_custom_call" | custom-call | tf_op jit(solution)/shard_map/pallas_call | solution.py:536
  132.1 1.7 %copy.15 = bf16[1,1,128,1024]{3,2,1,0:T(8,128)(2,1)} copy(bf16[1,1,128,1024]{3,2,1,0:T(8,128)(2,1)} %bitcast.10) | data formatting | bytes 524288

commit v5 on v4

--- a/solution.py
+++ b/solution.py
@@ -72,8 +72,8 @@
     def greet(**target):
         pl.semaphore_signal(barrier, inc=1, device_id=target, device_id_type=MESH)
 
+    load(patches_hbm, patches, 1).start()
     load(w_in_hbm, w_in, 0).start()
-    load(patches_hbm, patches, 1).start()
     for partner in (ahead, behind, sibling):
         greet(mp=partner)
 
@@ -116,29 +116,6 @@
         w_out_fetch(chip_pos).start()
     for chip_pos in range(n_ring):
         w_out_own(chip_pos).start()
-
-    position = lax.broadcasted_iota(jnp.int32, (seq_len, 1), 0)
-    group = position // per_group
-    owner = section * n_dp + dp
-    slots = owner * per_group + lax.rem(position, per_group)
-
-    def by_group(ref):
-        values = jnp.broadcast_to(ref[0:1, :], (seq_len, ref.shape[1]))
-        for e in range(1, n_dp):
-            values = jnp.where(group == e, ref[e : e + 1, :], values)
-        return values
-
-    _, covered = place(slots, by_group(sizes_ref), by_group(places_ref), by_group(offsets_ref))
-    text[...] = jnp.where(covered, jnp.zeros((), F32), text_ref[...].astype(F32)).astype(BF16)
-
-    everywhere = lax.broadcasted_iota(jnp.int32, (n_section * n_dp * per_group, 1), 0)
-    mine = pl.ds(dp, 1)
-    row, covered = place(everywhere, sizes_ref[mine, :], places_ref[mine, :], offsets_ref[mine, :])
-    candidates = lax.broadcasted_iota(jnp.int32, (everywhere.shape[0], rows_enc), 1)
-    picks[...] = jnp.where((candidates == row) & covered, 1.0, 0.0).astype(BF16)
-
-    for idx in range(n_mp):
-        load_weight(idx).start()
 
     def one_row(ref, begin, count):
         return jnp.concatenate([ref[pl.ds(begin + k, 1), :] for k in range(count)], axis=1)
@@ -240,6 +217,32 @@
     for p in range(PARTS):
         for h in range(2):
             own[h, :, p * span : (p + 1) * span] = partial(h, spot(h, 0), p)
+
+    for idx in range(n_mp):
+        load_weight(idx).start()
+
+    tall[...] = jnp.zeros_like(tall)
+
+    position = lax.broadcasted_iota(jnp.int32, (seq_len, 1), 0)
+    group = position // per_group
+    owner = section * n_dp + dp
+    slots = owner * per_group + lax.rem(position, per_group)
+
+    def by_group(ref):
+        values = jnp.broadcast_to(ref[0:1, :], (seq_len, ref.shape[1]))
+        for e in range(1, n_dp):
+            values = jnp.where(group == e, ref[e : e + 1, :], values)
+        return values
+
+    _, covered = place(slots, by_group(sizes_ref), by_group(places_ref), by_group(offsets_ref))
+    text[...] = jnp.where(covered, jnp.zeros((), F32), text_ref[...].astype(F32)).astype(BF16)
+
+    everywhere = lax.broadcasted_iota(jnp.int32, (n_section * n_dp * per_group, 1), 0)
+    mine = pl.ds(dp, 1)
+    row, covered = place(everywhere, sizes_ref[mine, :], places_ref[mine, :], offsets_ref[mine, :])
+    candidates = lax.broadcasted_iota(jnp.int32, (everywhere.shape[0], rows_enc), 1)
+    picks[...] = jnp.where((candidates == row) & covered, 1.0, 0.0).astype(BF16)
+
     for p in range(PARTS):
         for h in range(2):
             columns = slice(p * span, (p + 1) * span)
@@ -390,8 +393,6 @@
         total[...] = update if first else total[...] + update
 
     last = n_section - 1
-    tall[...] = jnp.zeros_like(tall)
-
     def begin(t):
         @pl.when(section == 0)
         def _():

time: 134 us -> 134 us (level)
  no operation moved by 1% of the time
where the time goes in v5:
time: 134 us; the launch traced here: 133 us
  Pallas kernels  132 us (99%)
  local copies, waits for them, and re-layouts  1.67 us (1%)
    pallas_call x1, Pallas kernels, per_device(): pl.pallas_call(kernel, out_shape=jax.ShapeDtypeStruct((seq_len, width), B...  132 us

profile of v5, /device:TPU:31, one launch (start us, length us, event | category | flops | bytes accessed | tf_op | source)
XLA Modules:
  0.0 133.4 jit_solution(12289909909797780638)
XLA Ops:
  0.0 131.7 %shard_map.127 = bf16[128,1024]{1,0:T(8,128)(2,1)} custom-call(bf16[256,5120]{1,0:T(8,128)(2,1)} %patches_hbm.1, f32[10,128]{1,0:T(8,128)} %bitcast.13, f32[10,128]{1,0:T(8,128)} %bitcast.14, bf16[160,5120]{1,0:T(8,128)(2,1)} %bitcast.9, f32[1,160]{1,0:T(1,128)} %bitcast.15, bf16[160,8192]{1,0:T(8,128)(2,1)} %w_out_hbm.1, f32[64,128]{1,0:T(8,128)} %bitcast.12, ...), custom_call_target="tpu_custom_call" | custom-call | tf_op jit(solution)/shard_map/pallas_call | solution.py:537
  131.7 1.7 %copy.15 = bf16[1,1,128,1024]{3,2,1,0:T(8,128)(2,1)} copy(bf16[1,1,128,1024]{3,2,1,0:T(8,128)(2,1)} %bitcast.10) | data formatting | bytes 524288

commit v6 on v5

--- a/solution.py
+++ b/solution.py
@@ -334,22 +334,24 @@
 
     def shard_copy(t, step, slot):
         return pltpu.make_async_remote_copy(
-            src_ref=shards.at[t, core, chip], dst_ref=shards.at[t, core, chip],
+            src_ref=shards.at[t, core, 0], dst_ref=shards.at[t, core, slot + 1],
             send_sem=sent.at[t, slot], recv_sem=got.at[t, slot],
             device_id={"mp": at(chip + step * turn, core)}, device_id_type=MESH,
         )
 
     def entry(t):
         return pltpu.make_async_remote_copy(
-            src_ref=results.at[t], dst_ref=shards.at[t, core, chip],
+            src_ref=results.at[t], dst_ref=shards.at[t, core, 0],
             send_sem=sent.at[t, 4], recv_sem=got.at[t, 4],
             device_id={"section": lax.rem(section + 1, n_section)}, device_id_type=MESH,
         )
 
-    def lend(t):
-        return pltpu.make_async_remote_copy(
-            src_ref=shards.at[t, core], dst_ref=shards.at[t, core],
-            send_sem=sent.at[t, 3], recv_sem=got.at[t, 3],
+    def lend(t, late):
+        those = pl.ds(3, 1) if late else pl.ds(0, 3)
+        slot = 5 if late else 3
+        return pltpu.make_async_remote_copy(
+            src_ref=shards.at[t, core, those], dst_ref=shards.at[t, core, those],
+            send_sem=sent.at[t, slot], recv_sem=got.at[t, slot],
             device_id={"mp": sibling}, device_id_type=MESH,
         )
 
@@ -369,7 +371,7 @@
             send_sem=text_sent, recv_sem=image_got.at[t],
             device_id={"section": 0}, device_id_type=MESH,
         ).wait_recv()
-        shards[t, core, chip] = (images[micro, here, :].astype(F32) + texts[micro, here, :].astype(F32)).astype(BF16)
+        shards[t, core, 0] = (images[micro, here, :].astype(F32) + texts[micro, here, :].astype(F32)).astype(BF16)
 
     def bring_home(t):
         half = lax.rem(t, per_micro)
@@ -379,17 +381,21 @@
             device_id={"section": t // per_micro}, device_id_type=MESH,
         )
 
-    def add(t, core_pos, chip_pos, first=False):
-        idx = chip_pos * 2 + core_pos
-        values = shards[t, core_pos, chip_pos].astype(F32)
+    def add(t, other, place):
+        step = (0, 1, -1, 2)[place]
+        core_pos = 1 - core if other else core
+        idx = ring(step if other else -step) * 2 + core_pos
+        first = not other and place == 0
+        spare = place + 4 * other
+        values = shards[t, core_pos, place].astype(F32)
         square = values * values
         lanes = square[:, :128] if first else squares[...] + square[:, :128]
         for j in range(128, width, 128):
             lanes = lanes + square[:, j : j + 128]
         squares[...] = lanes
         gain = gain_ref[:, pl.ds(pl.multiple_of(idx * width, width), width)]
-        tall[idx, 0:rows] = (values * gain).astype(BF16)
-        update = jnp.dot(tall[idx], weight[idx], preferred_element_type=F32)[0:rows]
+        tall[spare, 0:rows] = (values * gain).astype(BF16)
+        update = jnp.dot(tall[spare], weight[idx], preferred_element_type=F32)[0:rows]
         total[...] = update if first else total[...] + update
 
     last = n_section - 1
@@ -406,20 +412,23 @@
         shard_copy(t, -1, 1).start()
         shard_copy(t, 2, 2).start()
 
-    def share(t):
-        for slot in range(3):
+    def multiply(t):
+        for slot in range(2):
             shard_copy(t, 1, slot).wait_recv()
-        lend(t).start()
-
-    def multiply(t):
-        for step in range(n_ring):
-            add(t, core, ring(step), step == 0)
-        lend(t).wait_recv()
-        for step in range(n_ring):
-            add(t, 1 - core, ring(step))
+        lend(t, 0).start()
+        for place in range(3):
+            add(t, 0, place)
+        shard_copy(t, 1, 2).wait_recv()
+        lend(t, 1).start()
+        add(t, 0, 3)
+        lend(t, 0).wait_recv()
+        for place in range(3):
+            add(t, 1, place)
+        lend(t, 1).wait_recv()
+        add(t, 1, 3)
         square = jnp.sum(squares[...], axis=-1, keepdims=True) * (1.0 / (n_mp * width))
         update = total[...] * lax.rsqrt(square + 1e-06)
-        result = (shards[t, core, chip].astype(F32) + update).astype(BF16)
+        result = (shards[t, core, 0].astype(F32) + update).astype(BF16)
         results[t] = result
 
         @pl.when(section < last)
@@ -456,7 +465,6 @@
 
         @pl.when(t >= 0)
         def _():
-            share(t)
             multiply(t)
 
         return carry
@@ -493,7 +501,8 @@
     def settle(t, carry):
         for slot in range(3):
             shard_copy(t, 1, slot).wait_send()
-        lend(t).wait_send()
+        for late in range(2):
+            lend(t, late).wait_send()
 
         @pl.when((section < last) | (t < last * per_micro))
         def _():
@@ -575,8 +584,8 @@
             dma((n_section, n_dp)),
             dma((chunks,)),
             dma((n_mp,)),
-            dma((chunks, 5)),
-            dma((chunks, 5)),
+            dma((chunks, 6)),
+            dma((chunks, 6)),
             dma((per_micro,)),
         ],
         compiler_params=pltpu.CompilerParams(

time: 134 us -> 138 us (1.030)
  Pallas kernels: 132 us -> 136 us
    pallas_call x1, Pallas kernels: 132 us -> 136 us  [per_device(): pl.pallas_call(kernel, out_shape=jax.ShapeDtypeStruct((seq_len, width), B...]
where the time goes in v6:
time: 138 us; the launch traced here: 137 us
  Pallas kernels  136 us (99%)
  local copies, waits for them, and re-layouts  1.67 us (1%)
    pallas_call x1, Pallas kernels, per_device(): pl.pallas_call(kernel, out_shape=jax.ShapeDtypeStruct((seq_len, width), B...  136 us

profile of v6, /device:TPU:31, one launch (start us, length us, event | category | flops | bytes accessed | tf_op | source)
XLA Modules:
  0.0 137.5 jit_solution(5552325024422621797)
XLA Ops:
  0.0 135.8 %shard_map.127 = bf16[128,1024]{1,0:T(8,128)(2,1)} custom-call(bf16[256,5120]{1,0:T(8,128)(2,1)} %patches_hbm.1, f32[10,128]{1,0:T(8,128)} %bitcast.13, f32[10,128]{1,0:T(8,128)} %bitcast.14, bf16[160,5120]{1,0:T(8,128)(2,1)} %bitcast.9, f32[1,160]{1,0:T(1,128)} %bitcast.15, bf16[160,8192]{1,0:T(8,128)(2,1)} %w_out_hbm.1, f32[64,128]{1,0:T(8,128)} %bitcast.12, ...), custom_call_target="tpu_custom_call" | custom-call | tf_op jit(solution)/shard_map/pallas_call | solution.py:546
  135.8 1.7 %copy.15 = bf16[1,1,128,1024]{3,2,1,0:T(8,128)(2,1)} copy(bf16[1,1,128,1024]{3,2,1,0:T(8,128)(2,1)} %bitcast.10) | data formatting | bytes 524288

commit v7 on v5

--- a/solution.py
+++ b/solution.py
@@ -379,7 +379,8 @@
             device_id={"section": t // per_micro}, device_id_type=MESH,
         )
 
-    def add(t, core_pos, chip_pos, first=False):
+    def add(t, core_pos, chip_pos, spare):
+        first = spare == 0
         idx = chip_pos * 2 + core_pos
         values = shards[t, core_pos, chip_pos].astype(F32)
         square = values * values
@@ -388,8 +389,8 @@
             lanes = lanes + square[:, j : j + 128]
         squares[...] = lanes
         gain = gain_ref[:, pl.ds(pl.multiple_of(idx * width, width), width)]
-        tall[idx, 0:rows] = (values * gain).astype(BF16)
-        update = jnp.dot(tall[idx], weight[idx], preferred_element_type=F32)[0:rows]
+        tall[spare, 0:rows] = (values * gain).astype(BF16)
+        update = jnp.dot(tall[spare], weight[idx], preferred_element_type=F32)[0:rows]
         total[...] = update if first else total[...] + update
 
     last = n_section - 1
@@ -402,9 +403,9 @@
         def _():
             entry(t).wait_recv()
 
+        shard_copy(t, 2, 2).start()
         shard_copy(t, 1, 0).start()
         shard_copy(t, -1, 1).start()
-        shard_copy(t, 2, 2).start()
 
     def share(t):
         for slot in range(3):
@@ -413,10 +414,10 @@
 
     def multiply(t):
         for step in range(n_ring):
-            add(t, core, ring(step), step == 0)
+            add(t, core, ring(step), step)
         lend(t).wait_recv()
         for step in range(n_ring):
-            add(t, 1 - core, ring(step))
+            add(t, 1 - core, ring(step), n_ring + step)
         square = jnp.sum(squares[...], axis=-1, keepdims=True) * (1.0 / (n_mp * width))
         update = total[...] * lax.rsqrt(square + 1e-06)
         result = (shards[t, core, chip].astype(F32) + update).astype(BF16)
@@ -456,8 +457,11 @@
 
         @pl.when(t >= 0)
         def _():
-            share(t)
             multiply(t)
+
+        @pl.when((i >= LAG - 1) & (i < chunks + LAG - 1))
+        def _():
+            share(t + 1)
 
         return carry
 

time: 134 us -> 134 us (level)
  no operation moved by 1% of the time
where the time goes in v7:
time: 134 us; the launch traced here: 133 us
  Pallas kernels  132 us (99%)
  local copies, waits for them, and re-layouts  1.67 us (1%)
    pallas_call x1, Pallas kernels, per_device(): pl.pallas_call(kernel, out_shape=jax.ShapeDtypeStruct((seq_len, width), B...  132 us

profile of v7, /device:TPU:31, one launch (start us, length us, event | category | flops | bytes accessed | tf_op | source)
XLA Modules:
  0.0 133.4 jit_solution(10342479752841533849)
XLA Ops:
  0.0 131.7 %shard_map.127 = bf16[128,1024]{1,0:T(8,128)(2,1)} custom-call(bf16[256,5120]{1,0:T(8,128)(2,1)} %patches_hbm.1, f32[10,128]{1,0:T(8,128)} %bitcast.13, f32[10,128]{1,0:T(8,128)} %bitcast.14, bf16[160,5120]{1,0:T(8,128)(2,1)} %bitcast.9, f32[1,160]{1,0:T(1,128)} %bitcast.15, bf16[160,8192]{1,0:T(8,128)(2,1)} %w_out_hbm.1, f32[64,128]{1,0:T(8,128)} %bitcast.12, ...), custom_call_target="tpu_custom_call" | custom-call | tf_op jit(solution)/shard_map/pallas_call | solution.py:541
  131.7 1.7 %copy.15 = bf16[1,1,128,1024]{3,2,1,0:T(8,128)(2,1)} copy(bf16[1,1,128,1024]{3,2,1,0:T(8,128)(2,1)} %bitcast.10) | data formatting | bytes 524288

commit v8 on v7

--- a/solution.py
+++ b/solution.py
@@ -137,17 +137,17 @@
         return carry
 
     lax.fori_loop(0, rows_enc // block, norm, 0)
-    pl.semaphore_wait(barrier, jnp.where(section == 0, n_section * n_dp + 2, n_dp + n_section + 1))
-
-    for chip_pos in range(n_ring):
-        w_out_fetch(chip_pos).wait()
-        w_out_other(chip_pos).start()
-
     load(w_in_hbm, w_in, 0).wait()
     before = lax.dot_general(
         encoded[...], w_in[...], (((1,), (1,)), ((), ())), preferred_element_type=F32
     ) + b_in_ref[...]
     hidden[0] = (0.5 * before * (1.0 + lax.erf(before * (0.5**0.5)))).astype(BF16)
+
+    pl.semaphore_wait(barrier, jnp.where(section == 0, n_section * n_dp + 2, n_dp + n_section + 1))
+
+    for chip_pos in range(n_ring):
+        w_out_fetch(chip_pos).wait()
+        w_out_other(chip_pos).start()
 
     swap = pltpu.make_async_remote_copy(
         src_ref=hidden.at[0], dst_ref=hidden.at[1], send_sem=hid_sem.at[0], recv_sem=hid_sem.at[1],
@@ -457,11 +457,8 @@
 
         @pl.when(t >= 0)
         def _():
+            share(t)
             multiply(t)
-
-        @pl.when((i >= LAG - 1) & (i < chunks + LAG - 1))
-        def _():
-            share(t + 1)
 
         return carry
 

time: 134 us -> 136 us (1.015)
  Pallas kernels: 132 us -> 134 us
    pallas_call x1, Pallas kernels: 132 us -> 134 us  [per_device(): pl.pallas_call(kernel, out_shape=jax.ShapeDtypeStruct((seq_len, width), B...]
where the time goes in v8:
time: 136 us
  Pallas kernels  134 us (99%)
  local copies, waits for them, and re-layouts  1.67 us (1%)
    pallas_call x1, Pallas kernels, per_device(): pl.pallas_call(kernel, out_shape=jax.ShapeDtypeStruct((seq_len, width), B...  134 us

profile of v8, /device:TPU:31, one launch (start us, length us, event | category | flops | bytes accessed | tf_op | source)
XLA Modules:
  0.0 136.2 jit_solution(8428835720876196536)
XLA Ops:
  0.0 134.5 %shard_map.127 = bf16[128,1024]{1,0:T(8,128)(2,1)} custom-call(bf16[256,5120]{1,0:T(8,128)(2,1)} %patches_hbm.1, f32[10,128]{1,0:T(8,128)} %bitcast.13, f32[10,128]{1,0:T(8,128)} %bitcast.14, bf16[160,5120]{1,0:T(8,128)(2,1)} %bitcast.9, f32[1,160]{1,0:T(1,128)} %bitcast.15, bf16[160,8192]{1,0:T(8,128)(2,1)} %w_out_hbm.1, f32[64,128]{1,0:T(8,128)} %bitcast.12, ...), custom_call_target="tpu_custom_call" | custom-call | tf_op jit(solution)/shard_map/pallas_call | solution.py:538
  134.5 1.7 %copy.15 = bf16[1,1,128,1024]{3,2,1,0:T(8,128)(2,1)} copy(bf16[1,1,128,1024]{3,2,1,0:T(8,128)(2,1)} %bitcast.10) | data formatting | bytes 524288
